TPU v7x, 32 devices: a whole 2x2x4 slice. The times are simulated.
32 devices in a mesh: batch: 16 (over z, y, x), mp: 2 (over core).
Axes of the slice: x: 2, y: 2, z: 4, core: 2. Of those that a mesh axis runs over, the one named last changes fastest.
Arguments:
- features: bfloat16 [131072, 512], P('batch'), may hold values from -67 to 67, as said below
- validity: int32 [131072], P('batch'), may hold values from 0 to 1, as said below
- labels: int32 [131072, 2], P('batch'), may hold values from 0 to 1
- expert_in: float32 [6, 512, 256], P(None, None, 'mp'), may hold values from -0.25 to 0.25
- expert_in_bias: float32 [6, 256], P(None, 'mp'), may hold values from -2 to 2
- norm_gain: float32 [6, 256], P(None, 'mp'), may hold values from 0.25 to 1.75
- norm_bias: float32 [6, 256], P(None, 'mp'), may hold values from -2 to 2
- expert_out: float32 [6, 256, 256], P(None, 'mp'), may hold values from -0.375 to 0.375
- expert_out_bias: float32 [6, 256], replicated, may hold values from -2 to 2
- gate_weight: float32 [2, 512, 4], replicated, may hold values from -0.25 to 0.25
- gate_bias: float32 [2, 4], replicated, may hold values from -0.1 to 0.1
- tower_first: float32 [2, 256, 128], replicated, may hold values from -0.375 to 0.375
- tower_first_bias: float32 [2, 128], replicated, may hold values from -2 to 2
- tower_second: float32 [2, 128, 64], replicated, may hold values from -0.5 to 0.5
- tower_second_bias: float32 [2, 64], replicated, may hold values from -2 to 2
- tower_last: float32 [2, 64], replicated, may hold values from -0.75 to 0.75
- tower_last_bias: float32 [2], replicated, may hold values from -2 to 2
Outputs:
- predictions: float32 [131072, 2], P('batch')
- features_grad: float32 [131072, 512], P('batch', 'mp')
- grad_expert_in: float32 [6, 512, 256], P(None, None, 'mp')
- grad_expert_in_bias: float32 [6, 256], P(None, 'mp')
- grad_norm_gain: float32 [6, 256], P(None, 'mp')
- grad_norm_bias: float32 [6, 256], P(None, 'mp')
- grad_expert_out: float32 [6, 256, 256], P(None, 'mp')
- grad_expert_out_bias: float32 [6, 256], replicated
- grad_gate_weight: float32 [2, 512, 4], replicated
- grad_gate_bias: float32 [2, 4], replicated
- grad_tower_first: float32 [2, 256, 128], replicated
- grad_tower_first_bias: float32 [2, 128], replicated
- grad_tower_second: float32 [2, 128, 64], replicated
- grad_tower_second_bias: float32 [2, 64], replicated
- grad_tower_last: float32 [2, 64], replicated
- grad_tower_last_bias: float32 [2], replicated
Inputs may be any that keep to these rules, and one draw needn't show every extreme that they name: The features have a per-feature offset and scale. `validity`: each index of batch holds between 2048 and 8192 valid events; low indices tend to hold fewer than high ones, but neighbouring indices may be in either order.
All inputs are finite; a program needn't handle non-finite values.
Results may differ from a plain program's by a relative error of at most 0.0075.
Values may be sent and summed in bfloat16 or wider, within the bound.
A program may use at most 320 MiB of HBM per device.

v0:
```python
import jax
import jax.numpy as jnp
from jax import lax
from jax.sharding import PartitionSpec as P

TASKS = 2


EPS = 1e-05
HIGHEST = lax.Precision.HIGHEST
TASK_EXPERTS = ((0, 1, 4, 5), (2, 3, 4, 5))


def silu_slope(value):
    sigmoid_v = jax.nn.sigmoid(value)
    return sigmoid_v * (1.0 + value * (1.0 - sigmoid_v))


def on_device(
    features,
    validity,
    labels,
    expert_in,
    expert_in_bias,
    norm_gain,
    norm_bias,
    expert_out,
    expert_out_bias,
    gate_weight,
    gate_bias,
    tower_first,
    tower_first_bias,
    tower_second,
    tower_second_bias,
    tower_last,
    tower_last_bias,
):
    features_f = features.astype(jnp.float32)
    weight_matrix = validity.astype(jnp.float32)
    label_f = labels.astype(jnp.float32)
    mp_count = lax.axis_size("mp")
    parallel_rank_index = lax.axis_index("mp")
    local_hidden = expert_in.shape[2]
    full_hidden = local_hidden * mp_count
    shard_width = features_f.shape[1] // mp_count
    total_sum, overall_count = lax.psum(
        (jnp.sum(weight_matrix[:, None] * features_f, axis=0), jnp.sum(weight_matrix)), "batch"
    )
    mean_x = total_sum / overall_count
    mean_removed = features_f - mean_x
    total_square = lax.psum(
        jnp.sum(weight_matrix[:, None] * mean_removed * mean_removed, axis=0), "batch"
    )
    variance = total_square / overall_count
    inverse_deviation = lax.rsqrt(variance + EPS)
    standardized_input = mean_removed * inverse_deviation
    normed_rows = standardized_input.astype(jnp.bfloat16)
    in_low = expert_in.astype(jnp.bfloat16)
    out_low = expert_out.astype(jnp.bfloat16)
    gate_low = gate_weight.astype(jnp.bfloat16)
    pre_act = jnp.einsum("rd,edh->erh", normed_rows, in_low, preferred_element_type=jnp.float32)
    pre_act = pre_act + expert_in_bias[:, None, :]
    row_sum, row_square = lax.psum(
        (jnp.sum(pre_act, axis=-1), jnp.sum(pre_act * pre_act, axis=-1)), "mp"
    )
    row_mean = row_sum / full_hidden
    row_inv = lax.rsqrt(row_square / full_hidden - row_mean * row_mean + EPS)
    zhat = (pre_act - row_mean[:, :, None]) * row_inv[:, :, None]
    zvalue = zhat * norm_gain[:, None, :] + norm_bias[:, None, :]
    hidden_low = (zvalue * jax.nn.sigmoid(zvalue)).astype(jnp.bfloat16)
    partial_out = jnp.einsum(
        "erh,eho->ero", hidden_low, out_low, preferred_element_type=jnp.float32
    )
    own_part = lax.psum_scatter(partial_out, "mp", scatter_dimension=2, tiled=True)
    out_cols = own_part.shape[2]
    bias_part = lax.dynamic_slice_in_dim(
        expert_out_bias, parallel_rank_index * out_cols, out_cols, 1
    )
    own_low = (own_part + bias_part[:, None, :]).astype(jnp.bfloat16)
    outputs = lax.all_gather(own_low, "mp", axis=2, tiled=True)
    outputs_f = outputs.astype(jnp.float32)
    work_normed_f = normed_rows.astype(jnp.float32)
    logits = jnp.einsum("rd,tdk->trk", normed_rows, gate_low, preferred_element_type=jnp.float32)
    gate_prob = jax.nn.softmax(logits + gate_bias[:, None, :], axis=-1)
    d_outputs = [jnp.zeros_like(outputs_f[0]) for expert_id in range(outputs_f.shape[0])]
    predicted = []
    grad_gate_w, grad_gate_b = ([], [])
    grad_first, grad_first_b, grad_second, grad_second_b, grad_last, grad_last_b = (
        [],
        [],
        [],
        [],
        [],
        [],
    )
    d_normed = jnp.zeros_like(work_normed_f)
    for task_id in range(TASKS):
        experts_used = TASK_EXPERTS[task_id]
        mixed = jnp.zeros_like(outputs_f[0])
        for slot_id in range(4):
            mixed = mixed + gate_prob[task_id, :, slot_id, None] * outputs_f[experts_used[slot_id]]
        first_pre = (
            jnp.dot(mixed, tower_first[task_id], precision=HIGHEST) + tower_first_bias[task_id]
        )
        first_act = first_pre * jax.nn.sigmoid(first_pre)
        second_pre = (
            jnp.dot(first_act, tower_second[task_id], precision=HIGHEST)
            + tower_second_bias[task_id]
        )
        second_act = second_pre * jax.nn.sigmoid(second_pre)
        logit = (
            jnp.dot(second_act, tower_last[task_id], precision=HIGHEST) + tower_last_bias[task_id]
        )
        prob_task = jax.nn.sigmoid(logit)
        predicted.append(prob_task)
        d_logit = weight_matrix * (prob_task - label_f[:, task_id])
        grad_last.append(jnp.dot(d_logit, second_act, precision=HIGHEST))
        grad_last_b.append(jnp.sum(d_logit))
        d_second = d_logit[:, None] * tower_last[task_id][None, :] * silu_slope(second_pre)
        grad_second.append(jnp.dot(first_act.T, d_second, precision=HIGHEST))
        grad_second_b.append(jnp.sum(d_second, axis=0))
        d_first = jnp.dot(d_second, tower_second[task_id].T, precision=HIGHEST) * silu_slope(
            first_pre
        )
        grad_first.append(jnp.dot(mixed.T, d_first, precision=HIGHEST))
        grad_first_b.append(jnp.sum(d_first, axis=0))
        d_mixed = jnp.dot(d_first, tower_first[task_id].T, precision=HIGHEST)
        d_prob = []
        for slot_id in range(4):
            expert_id = experts_used[slot_id]
            d_outputs[expert_id] = (
                d_outputs[expert_id] + gate_prob[task_id, :, slot_id, None] * d_mixed
            )
            d_prob.append(jnp.sum(d_mixed * outputs_f[expert_id], axis=-1))
        d_prob = jnp.stack(d_prob, axis=1)
        prob_row = gate_prob[task_id]
        d_gate = prob_row * (d_prob - jnp.sum(prob_row * d_prob, axis=-1, keepdims=True))
        grad_gate_w.append(jnp.dot(work_normed_f.T, d_gate, precision=HIGHEST))
        grad_gate_b.append(jnp.sum(d_gate, axis=0))
        d_normed = d_normed + jnp.dot(
            d_gate, gate_low[task_id].astype(jnp.float32).T, precision=HIGHEST
        )
    head_terms = (
        jnp.stack(grad_gate_w),
        jnp.stack(grad_gate_b),
        jnp.stack(grad_first),
        jnp.stack(grad_first_b),
        jnp.stack(grad_second),
        jnp.stack(grad_second_b),
        jnp.stack(grad_last),
        jnp.stack(grad_last_b),
    )
    d_out_low = jnp.stack(d_outputs).astype(jnp.bfloat16)
    grad_out_w = jnp.einsum(
        "erh,ero->eho", hidden_low, d_out_low, preferred_element_type=jnp.float32
    )
    grad_out_b = jnp.sum(d_out_low.astype(jnp.float32), axis=1)
    d_hidden = jnp.einsum("ero,eho->erh", d_out_low, out_low, preferred_element_type=jnp.float32)
    d_zvalue = d_hidden * silu_slope(zvalue)
    grad_norm_b = jnp.sum(d_zvalue, axis=1)
    grad_norm_g = jnp.sum(d_zvalue * zhat, axis=1)
    d_zhat = d_zvalue * norm_gain[:, None, :]
    back_sum, back_cross = lax.psum(
        (jnp.sum(d_zhat, axis=-1), jnp.sum(d_zhat * zhat, axis=-1)), "mp"
    )
    d_pre = row_inv[:, :, None] * (
        d_zhat - back_sum[:, :, None] / full_hidden - zhat * back_cross[:, :, None] / full_hidden
    )
    d_pre_low = d_pre.astype(jnp.bfloat16)
    grad_in_b = jnp.sum(d_pre_low.astype(jnp.float32), axis=1)
    grad_in_w = jnp.einsum(
        "rd,erh->edh", normed_rows, d_pre_low, preferred_element_type=jnp.float32
    )
    d_normed_part = jnp.einsum("erh,edh->rd", d_pre_low, in_low, preferred_element_type=jnp.float32)
    normed_gradient_local = lax.psum_scatter(
        d_normed_part.astype(jnp.bfloat16), "mp", scatter_dimension=1, tiled=True
    ).astype(jnp.float32)
    normed_gradient_local = normed_gradient_local + lax.dynamic_slice_in_dim(
        d_normed, parallel_rank_index * shard_width, shard_width, 1
    )
    predictions = jnp.stack(predicted, axis=1)
    standardized_local = lax.dynamic_slice_in_dim(
        standardized_input, parallel_rank_index * shard_width, shard_width, 1
    )
    inv_own = lax.dynamic_slice_in_dim(
        inverse_deviation, parallel_rank_index * shard_width, shard_width, 0
    )
    gradient_total, cross_term_gradient = lax.psum(
        (
            jnp.sum(normed_gradient_local, axis=0),
            jnp.sum(normed_gradient_local * standardized_local, axis=0),
        ),
        "batch",
    )
    features_grad = inv_own * (
        normed_gradient_local
        - weight_matrix[:, None]
        / overall_count
        * (gradient_total + standardized_local * cross_term_gradient)
    )
    expert_terms = (grad_in_w, grad_in_b, grad_norm_g, grad_norm_b, grad_out_w, grad_out_b)
    summed_all = lax.psum(expert_terms + head_terms, "batch")
    expert_terms = summed_all[:6]
    head_terms = summed_all[6:]
    scaled = tuple((item / overall_count for item in expert_terms + head_terms))
    return (predictions, features_grad) + scaled


def solution(mesh):
    in_specs = (
        P("batch", None),
        P("batch"),
        P("batch", None),
        P(None, None, "mp"),
        P(None, "mp"),
        P(None, "mp"),
        P(None, "mp"),
        P(None, "mp", None),
        P(),
        P(),
        P(),
        P(),
        P(),
        P(),
        P(),
        P(),
        P(),
    )
    out_specs = (
        P("batch", None),
        P("batch", "mp"),
        P(None, None, "mp"),
        P(None, "mp"),
        P(None, "mp"),
        P(None, "mp"),
        P(None, "mp", None),
        P(),
        P(),
        P(),
        P(),
        P(),
        P(),
        P(),
        P(),
        P(),
    )
    return jax.shard_map(
        on_device, mesh=mesh, in_specs=in_specs, out_specs=out_specs, check_vma=False
    )
```

profile of v0, /device:TPU:0, one launch (start us, length us, event | category | flops | bytes accessed | tf_op | source)
XLA Modules:
  0.0 906.3 jit_solution(5399499088204429262)
XLA Ops:
  9.4 5.0 fusion.4
  14.4 44.2 %all-reduce.1 = (f32[512]{0:T(512)S(1)}, f32[]{:T(128)}) all-reduce(f32[512]{0:T(512)S(1)} %fusion.4, f32[]{:T(128)} %convert_reduce_fusion.2), channel_id=1, replica_groups=mesh['batch'=16,'mp'=2] {'batch'}, use_global_device_ids=true, to_apply=%region_1.0 | all-reduce | flops 513 | bytes 4104 | tf_op jit(solution)/shard_map/psum | solution.py:46
  59.3 5.5 fusion.5
  64.7 36.6 %psum.163 = f32[512]{0:T(512)S(1)} all-reduce(f32[512]{0:T(512)S(1)} %fusion.5), channel_id=1, replica_groups=mesh['batch'=16,'mp'=2] {'batch'}, use_global_device_ids=true, to_apply=%region_5.0 | all-reduce | flops 512 | bytes 4096 | tf_op jit(solution)/shard_map/psum | solution.py:51
  102.4 15.1 %fusion.114 = f32[8192,768]{0,1} fusion(bf16[512,768]{0,1:T(8,128)(2,1)S(1)} %bitcast.309, f32[512]{0:T(512)S(1)} %add_rsqrt_fusion.1, f32[512]{0:T(512)S(1)} %broadcast_divide_fusion.11, bf16[8192,512]{1,0:T(8,128)(2,1)} %param.17), kind=kOutput, calls=%fused_computation.158 | convolution fusion | flops 6459228160 | bytes 34344960
  117.5 11.3 %bitcast_reduce_fusion = (f32[6,8192]{1,0:T(8,128)}, f32[6,8192]{1,0:T(8,128)}) fusion(f32[8192,6,128]{0,2,1:T(8,128)} %bitcast.301, f32[6,128]{1,0:T(8,128)S(1)} %copy-done.32), kind=kLoop, calls=%fused_computation.4 | loop fusion | flops 25067520 | bytes 25562112 | tf_op jit(solution)/shard_map/reduce_sum | solution.py:64
  128.9 16.7 %all-reduce.13.cloned.1.call-done = (f32[6,8192]{1,0:T(8,128)}, f32[6,8192]{1,0:T(8,128)}) async-done(((f32[6,8192]{1,0:T(8,128)}, f32[6,8192]{1,0:T(8,128)}), (f32[6,8192]{1,0:T(8,128)}, f32[6,8192]{1,0:T(8,128)})) %all-reduce.13.cloned.1.call-update) | async-done | bytes 393232 | tf_op jit(solution)/shard_map/psum | solution.py:63
  147.5 17.5 %multiply_convert_fusion.1 = bf16[6,8192,128]{1,2,0:T(8,128)(2,1)} fusion(f32[6,128]{1,0:T(8,128)S(1)} %copy-done.44, f32[6,128]{1,0:T(8,128)S(1)} %copy-done.39, f32[6,8192]{1,0:T(8,128)S(1)} %get-tuple-element.100, f32[6,8192]{1,0:T(8,128)S(1)} %get-tuple-element.99, f32[8192,6,128]{0,2,1:T(8,128)} %bitcast.302, f32[6,128]{1,0:T(8,128)S(1)} %copy-done.32), kind=kLoop, calls=%fused_computation.13 | loop fusion | flops 62914560 | bytes 38151168 | tf_op jit(solution)/shard_map/convert_element_type | solution.py:70
  165.0 21.7 %fusion.126 = f32[6,8192,256]{2,1,0:T(8,128)} fusion(bf16[6,8192,128]{1,2,0:T(8,128)(2,1)} %multiply_convert_fusion.1, f32[6,128,256]{2,1,0:T(8,128)S(1)} %copy-done.15), kind=kOutput, calls=%fused_computation.167 | convolution fusion | flops 3221422080 | bytes 63700992 | tf_op jit(solution)/shard_map/erh,eho->ero/dot_general | solution.py:71
  186.8 64.6 %reduce-scatter.3.cloned.1.call-done = f32[6,8192,128]{2,1,0:T(8,128)} async-done(((f32[6,8192,256]{2,1,0:T(8,128)}), f32[6,8192,128]{2,1,0:T(8,128)}) %reduce-scatter.3.cloned.1.call-update) | async-done | bytes 25165840 | tf_op jit(solution)/shard_map/reduce_scatter | solution.py:74
  251.5 13.1 %add_convert_fusion = bf16[6,8192,128]{2,1,0:T(8,128)(2,1)} fusion(f32[6,8192,128]{2,1,0:T(8,128)} %reduce-scatter.3.cloned.1.call-done, f32[6,128]{1,0:T(8,128)S(1)} %constant_dynamic-slice_fusion), kind=kLoop, calls=%fused_computation.12 | loop fusion | flops 12582912 | bytes 37751808 | tf_op jit(solution)/shard_map/convert_element_type | solution.py:79
  266.1 5.8 fusion.197
  273.0 33.2 %all-gather.2.cloned.1.call-done = bf16[6,8192,256]{2,1,0:T(8,128)(2,1)} async-done(((bf16[6,8192,128]{2,1,0:T(8,128)(2,1)}), bf16[6,8192,256]{2,1,0:T(8,128)(2,1)}) %all-gather.2.cloned.1.call-update) | async-done | bytes 25165840 | tf_op jit(solution)/shard_map/all_gather | solution.py:80
  306.2 27.1 %convert_element_type.57 = f32[6,8192,256]{2,1,0:T(8,128)} convert(bf16[6,8192,256]{2,1,0:T(8,128)(2,1)} %all-gather.2.cloned.1.call-done) | non-fusion elementwise | flops 12582912 | bytes 75497472 | tf_op jit(solution)/shard_map/convert_element_type | solution.py:81
  333.3 18.3 %convolution_add_fusion = f32[8192,128]{1,0:T(8,128)S(1)} fusion(f32[6,8192,256]{2,1,0:T(8,128)} %convert_element_type.57, f32[8192]{0:T(1024)S(1)} %bitcast.336, f32[8192]{0:T(1024)S(1)} %bitcast.342, f32[8192]{0:T(1024)S(1)} %bitcast.348, f32[8192]{0:T(1024)S(1)} %bitcast.351, f32[128]{0:T(128)S(1)} %get-tuple-element.110, f32[2,256,128]{2,1,0:T(8,128)S(1)} %copy-done.30), kind=kOutput, calls=%fused_computation.26 | convolution fusion | flops 3236954112 | bytes 38011392 | tf_op jit(solution)/shard_map/dot_general | solution.py:103
  351.7 5.6 convolution_add_fusion.2
  358.9 18.5 %convolution_add_fusion.1 = f32[8192,128]{1,0:T(8,128)S(1)} fusion(f32[6,8192,256]{2,1,0:T(8,128)} %convert_element_type.57, f32[8192]{0:T(1024)S(1)} %bitcast.339, f32[8192]{0:T(1024)S(1)} %bitcast.345, f32[8192]{0:T(1024)S(1)} %bitcast.354, f32[8192]{0:T(1024)S(1)} %bitcast.357, f32[128]{0:T(128)S(1)} %get-tuple-element.109, f32[2,256,128]{2,1,0:T(8,128)S(1)} %copy-done.30), kind=kOutput, calls=%fused_computation.27 | convolution fusion | flops 3236954112 | bytes 38011392 | tf_op jit(solution)/shard_map/dot_general | solution.py:103
  377.4 5.6 convolution_add_fusion.3
  384.6 3.2 fusion.189
  387.8 4.9 convolution_bitcast_fusion.1
  392.7 8.7 fusion.199
  401.4 8.5 fusion.198
  409.9 24.1 %fusion.104 = f32[1,256,128]{2,1,0:T(8,128)S(1)} fusion(f32[8192,128]{1,0:T(8,128)S(1)} %get-tuple-element.120, f32[6,8192,256]{2,1,0:T(8,128)} %convert_element_type.57, f32[8192]{0:T(1024)S(1)} %bitcast.337, f32[8192]{0:T(1024)S(1)} %bitcast.343, f32[8192]{0:T(1024)S(1)} %bitcast.349, f32[8192]{0:T(1024)S(1)} %bitcast.352), kind=kOutput, calls=%fused_computation.152 | convolution fusion | flops 3235905536 | bytes 38010880 | tf_op jit(solution)/shard_map/dot_general | solution.py:125
  434.0 8.9 fusion.150
  442.9 24.1 %fusion.101 = f32[1,256,128]{2,1,0:T(8,128)S(1)} fusion(f32[8192,128]{1,0:T(8,128)S(1)} %get-tuple-element.122, f32[6,8192,256]{2,1,0:T(8,128)} %convert_element_type.57, f32[8192]{0:T(1024)S(1)} %bitcast.340, f32[8192]{0:T(1024)S(1)} %bitcast.346, f32[8192]{0:T(1024)S(1)} %bitcast.355, f32[8192]{0:T(1024)S(1)} %bitcast.358), kind=kOutput, calls=%fused_computation.151 | convolution fusion | flops 3235905536 | bytes 38010880 | tf_op jit(solution)/shard_map/dot_general | solution.py:125
  467.1 27.5 %fusion.29 = (f32[8192]{0:T(1024)}, f32[8192]{0:T(1024)}, f32[8192]{0:T(1024)}, f32[8192]{0:T(1024)}, f32[8192]{0:T(1024)}, /*index=5*/f32[8192]{0:T(1024)}, f32[8192]{0:T(1024)}, f32[8192]{0:T(1024)}, f32[8192,256]{1,0:T(8,128)}) fusion(f32[6,8192,256]{2,1,0:T(8,128)} %convert_element_type.57, f32[8192,256]{1,0:T(8,128)} %fusion.150, ...), kind=kOutput, calls=%fused_computation.67 | convolution fusion | flops 3254714368 | bytes 71696384 | tf_op jit(solution)/shard_map/dot_general | solution.py:127
  494.6 5.7 fusion.66
  511.3 5.3 fusion.74
  516.6 5.3 fusion.76
  521.9 16.1 %fusion.202 = f32[6,128,256]{2,1,0:T(8,128)} fusion(bf16[6,8192,128]{1,2,0:T(8,128)(2,1)} %multiply_convert_fusion.1, bf16[6,8192,256]{2,1,0:T(8,128)(2,1)} %fusion.76), kind=kOutput, calls=%fused_computation.286 | convolution fusion | flops 3221225472 | bytes 38535168 | tf_op jit(solution)/shard_map/erh,ero->eho/dot_general | solution.py:154
  538.0 32.4 %multiply_reduce_fusion = (f32[6,128]{1,0:T(8,128)S(1)}, f32[6,8192]{1,0:T(8,128)}, f32[6,8192]{1,0:T(8,128)}, f32[6,128]{1,0:T(8,128)S(1)}, f32[6,8192,128]{1,2,0:T(8,128)}) fusion(f32[6,8192]{1,0:T(8,128)S(1)} %copy-done.11, f32[6,8192]{1,0:T(8,128)S(1)} %copy-done.9, f32[8192,6,128]{0,2,1:T(8,128)} %bitcast.303, f32[6,128]{1,0:T(8,128)S(1)} %copy-done.33, ...), kind=kOutput, calls=%fused_computation.7 | convolution fusion | flops 3347151360 | bytes 77085696 | tf_op jit(solution)/shard_map/ero,eho->erh/dot_general | solution.py:158
  570.5 6.1 convolution_bitcast_fusion
  577.9 12.6 %all-reduce.11.cloned.1.call-done = (f32[6,8192]{1,0:T(8,128)}, f32[6,8192]{1,0:T(8,128)}) async-done(((f32[6,8192]{1,0:T(8,128)}, f32[6,8192]{1,0:T(8,128)}), (f32[6,8192]{1,0:T(8,128)}, f32[6,8192]{1,0:T(8,128)})) %all-reduce.11.cloned.1.call-update) | async-done | bytes 393232 | tf_op jit(solution)/shard_map/psum | solution.py:163
  591.6 19.9 %convert_reduce_fusion.1 = (f32[6,128]{1,0:T(8,128)S(1)}, bf16[6,8192,128]{1,2,0:T(8,128)(2,1)S(1)}) fusion(f32[6,8192]{1,0:T(8,128)} %get-tuple-element.72, f32[6,8192]{1,0:T(8,128)S(1)} %copy-done.9, f32[8192,6,128]{0,2,1:T(8,128)} %bitcast.304, f32[6,128]{1,0:T(8,128)S(1)} %copy-done.33, f32[6,8192]{1,0:T(8,128)S(1)} %broadcast_multiply_fusion, ...), kind=kLoop, calls=%fused_computation.8 | loop fusion | flops 75496704 | bytes 63710208 | tf_op jit(solution)/shard_map/reduce_sum | solution.py:170
  611.5 4.6 copy-done.3
  616.1 10.2 %fusion.98 = f32[6,512,128]{1,2,0:T(8,128)} fusion(bf16[6,8192,128]{1,2,0:T(8,128)(2,1)S(1)} %get-tuple-element.87, f32[512]{0:T(512)S(1)} %copy-done.43, f32[512]{0:T(512)S(1)} %copy-done.38, bf16[8192,512]{1,0:T(8,128)(2,1)} %param.17), kind=kOutput, calls=%fused_computation.150 | convolution fusion | flops 6459228160 | bytes 22548480 | tf_op jit(solution)/shard_map/rd,erh->edh/dot_general | solution.py:171
  626.4 14.1 %bitcast_convert_fusion = bf16[8192,512]{1,0:T(8,128)(2,1)} fusion(bf16[6,8192,128]{1,2,0:T(8,128)(2,1)} %copy-done.3, bf16[6,512,128]{2,1,0:T(8,128)(2,1)S(1)} %copy-done.7), kind=kOutput, calls=%fused_computation.23 | convolution fusion | flops 6446645248 | bytes 21757952 | tf_op jit(solution)/shard_map/erh,edh->rd/dot_general | solution.py:174
  640.6 11.8 %fusion.3 = f32[8192,512]{1,0:T(8,128)} fusion(bf16[8192,512]{1,0:T(8,128)(2,1)} %param.17, f32[512]{0:T(512)S(1)} %copy-done.43, f32[512]{0:T(512)S(1)} %copy-done.38), kind=kLoop, calls=%fused_computation.20 | loop fusion | flops 12582912 | bytes 25169920 | tf_op jit(solution)/shard_map/mul | solution.py:56
  660.4 4.2 convolution_bitcast_fusion.3
  664.6 4.4 convolution_bitcast_fusion.2
  669.1 10.3 %fusion.130 = f32[8192,512]{1,0:T(8,128)} fusion(f32[1,8192,1]{1,2,0:T(1,128)S(1)} %bitcast.333, f32[1,8192,1]{1,2,0:T(1,128)S(1)} %bitcast.327, f32[1,8192,1]{1,2,0:T(1,128)S(1)} %bitcast.330, f32[1,8192,1]{1,2,0:T(1,128)S(1)} %bitcast.324, f32[2,8192,4]{1,2,0:T(4,128)S(1)} %copy-done.5, f32[8192]{0:T(1024)S(1)} %get-tuple-element.52, ...), kind=kOutput, calls=%fused_computation.172 | convolution fusion | flops 201490432 | bytes 17076224 | tf_op jit(solution)/shard_map/dot_general | solution.py:140
  679.4 10.2 %fusion.140 = f32[8192,512]{1,0:T(8,128)} fusion(f32[1,8192,1]{1,2,0:T(1,128)S(1)} %bitcast.312, f32[1,8192,1]{1,2,0:T(1,128)S(1)} %bitcast.318, f32[1,8192,1]{1,2,0:T(1,128)S(1)} %bitcast.315, f32[1,8192,1]{1,2,0:T(1,128)S(1)} %bitcast.321, f32[2,8192,4]{1,2,0:T(4,128)S(1)} %copy-done.5, f32[8192]{0:T(1024)S(1)} %get-tuple-element.53, ...), kind=kOutput, calls=%fused_computation.183 | convolution fusion | flops 201490432 | bytes 17076224 | tf_op jit(solution)/shard_map/dot_general | solution.py:140
  690.4 13.1 %convert_reduce_fusion = f32[6,256]{1,0:T(8,128)S(1)} fusion(bf16[6,8192,256]{2,1,0:T(8,128)(2,1)S(1)} %bitcast.306), kind=kLoop, calls=%fused_computation.1 | loop fusion | flops 25164288 | bytes 25171968 | tf_op jit(solution)/shard_map/reduce_sum | solution.py:157
  703.5 63.0 %all-reduce.9.cloned.1.call-done = (f32[6,512,128]{1,2,0:T(8,128)}, f32[6,128,256]{2,1,0:T(8,128)}, f32[2,256,128]{2,1,0:T(8,128)}, f32[2,128,64]{1,2,0:T(8,128)}) async-done(((f32[6,512,128]{1,2,0:T(8,128)}, f32[6,128,256]{2,1,0:T(8,128)}, f32[2,256,128]{2,1,0:T(8,128)}, f32[2,128,64]{1,2,0:T(8,128)}), (f32[6,512,128]{1,2,0:T(8,128)}, f32[6,128,256]{2,1,0:T(8,128)}, f32[2,256,128]{2,1,0:T(8,128)}, ...) | async-done | bytes 2686992 | tf_op jit(solution)/shard_map/psum | solution.py:202
  777.4 8.3 reduce-scatter.5.cloned.1.call-done
  785.7 14.3 %fusion.188 = (f32[256]{0:T(256)S(1)}, f32[256]{0:T(256)S(1)}, f32[8192,256]{1,0:T(8,128)}) fusion(f32[8192,512]{1,0:T(8,128)} %fusion.3, s32[]{:T(128)S(6)} %select_n.9, f32[8192,512]{1,0:T(8,128)} %fusion.140, f32[8192,512]{1,0:T(8,128)} %fusion.130, bf16[8192,256]{1,0:T(8,128)(2,1)} %reduce-scatter.5.cloned.1.call-done), kind=kLoop, calls=%fused_computation.275 | loop fusion | flops 12582400 | bytes 37750788 | tf_op jit(solution)/shard_map/reduce_sum | solution.py:190
  800.0 77.2 %all-reduce = (f32[256]{0:T(256)S(1)}, f32[256]{0:T(256)S(1)}, f32[6,128]{1,0:T(8,128)S(1)}, f32[6,128]{1,0:T(8,128)S(1)}, f32[6,128]{1,0:T(8,128)S(1)}, /*index...) all-reduce(f32[256]{0:T(256)S(1)} %get-tuple-element.51, ...), channel_id=1, replica_groups=mesh['batch'=16,'mp'=2] {'batch'}, use_global_device_ids=true, to_apply=%region_31.0 | all-reduce | flops 8970 | bytes 71760 | tf_op jit(solution)/shard_map/psum | solution.py:188
  889.2 10.1 %subtract_multiply_fusion = f32[8192,256]{1,0:T(8,128)} fusion(f32[8192,256]{1,0:T(8,128)} %get-tuple-element.88, f32[8192,512]{1,0:T(8,128)} %fusion.3, s32[]{:T(128)S(6)} %select_n.9, f32[256]{0:T(256)S(1)} %get-tuple-element.54, f32[256]{0:T(256)S(1)} %get-tuple-element.55, f32[8192]{0:T(1024)S(1)} %copy-done.25, f32[256]{0:T(256)S(1)} %dynamic_slice.13), kind=kLoop, calls=%fused_computation.73 | loop fusion | flops 10485760 | bytes 25201668 | tf_op jit(solution)/shard_map/mul | solution.py:195
  (203 shorter events, 56.7 us)
Async XLA Ops:
  7.2 179.6 %copy-start = (f32[6,256]{1,0:T(8,128)S(1)}, f32[6,256]{1,0:T(8,128)}, u32[]{:S(2)}) copy-start(f32[6,256]{1,0:T(8,128)} %param.25) | copy-start | bytes 18436
  7.2 138.4 %all-reduce.13.cloned.1.call-start = ((), (), s32[]{:S(2)}) async-start(), calls=%async_computation.7 | async-start | bytes 1048576 | tf_op jit(solution)/shard_map/psum | solution.py:63
  9.4 92.6 %copy-start.14 = (f32[6,512,128]{2,1,0:T(8,128)S(1)}, f32[6,512,128]{2,1,0:T(8,128)}, u32[]{:S(2)}) copy-start(f32[6,512,128]{2,1,0:T(8,128)} %param.20) | copy-start | bytes 4718596
  59.2 206.8 %copy-start.37 = (f32[512]{0:T(512)}, f32[512]{0:T(512)S(1)}, u32[]{:S(2)}) copy-start(f32[512]{0:T(512)S(1)} %broadcast_divide_fusion.11) | copy-start | bytes 6148
  102.0 164.1 %copy-start.42 = (f32[512]{0:T(512)}, f32[512]{0:T(512)S(1)}, u32[]{:S(2)}) copy-start(f32[512]{0:T(512)S(1)} %add_rsqrt_fusion.1) | copy-start | bytes 6148
  102.1 15.4 %copy-start.6 = (bf16[6,512,128]{2,1,0:T(8,128)(2,1)}, bf16[6,512,128]{2,1,0:T(8,128)(2,1)S(1)}, u32[]{:S(2)}) copy-start(bf16[6,512,128]{2,1,0:T(8,128)(2,1)S(1)} %convert_element_type.53) | copy-start | bytes 2359300
  102.4 15.1 %copy-start.32 = (f32[6,128]{1,0:T(8,128)S(1)}, f32[6,128]{1,0:T(8,128)}, u32[]{:S(2)}) copy-start(f32[6,128]{1,0:T(8,128)} %param.21) | copy-start | bytes 9220
  117.5 30.0 %copy-start.39 = (f32[6,128]{1,0:T(8,128)S(1)}, f32[6,128]{1,0:T(8,128)}, u32[]{:S(2)}) copy-start(f32[6,128]{1,0:T(8,128)} %param.22) | copy-start | bytes 9220
  117.5 30.0 %copy-start.44 = (f32[6,128]{1,0:T(8,128)S(1)}, f32[6,128]{1,0:T(8,128)}, u32[]{:S(2)}) copy-start(f32[6,128]{1,0:T(8,128)} %param.23) | copy-start | bytes 9220
  128.9 122.6 %reduce-scatter.3.cloned.1.call-start = ((), (), s32[]{:S(2)}) async-start(), calls=%async_computation.2 | async-start | bytes 75497472 | tf_op jit(solution)/shard_map/reduce_scatter | solution.py:74
  147.5 17.5 %copy-start.15 = (f32[6,128,256]{2,1,0:T(8,128)S(1)}, f32[6,128,256]{2,1,0:T(8,128)}, u32[]{:S(2)}) copy-start(f32[6,128,256]{2,1,0:T(8,128)} %param.24) | copy-start | bytes 2359300
  186.8 119.4 %all-gather.2.cloned.1.call-start = ((), (), s32[]{:S(2)}) async-start(), calls=%async_computation.3 | async-start | bytes 37748736 | tf_op jit(solution)/shard_map/all_gather | solution.py:80
  264.6 325.9 %all-reduce.11.cloned.1.call-start = ((), (), s32[]{:S(2)}) async-start(), calls=%async_computation.6 | async-start | bytes 1048576 | tf_op jit(solution)/shard_map/psum | solution.py:163
  265.4 7.6 copy-start.35
  266.1 126.6 %copy-start.47 = (f32[64]{0:T(128)}, f32[64]{0:T(128)S(1)}, u32[]{:S(2)}) copy-start(f32[64]{0:T(128)S(1)} %get-tuple-element.108) | copy-start | bytes 772
  273.0 60.4 %copy-start.30 = (f32[2,256,128]{2,1,0:T(8,128)S(1)}, f32[2,256,128]{2,1,0:T(8,128)}, u32[]{:S(2)}) copy-start(f32[2,256,128]{2,1,0:T(8,128)} %param.28) | copy-start | bytes 786436
  333.3 18.4 %copy-start.54 = (f32[2,128,64]{1,2,0:T(8,128)S(1)}, f32[2,128,64]{1,2,0:T(8,128)}, u32[]{:S(2)}) copy-start(f32[2,128,64]{1,2,0:T(8,128)} %param.30) | copy-start | bytes 196612
  351.7 49.7 %copy-start.57 = (f32[8192,128]{1,0:T(8,128)}, f32[8192,128]{1,0:T(8,128)S(1)}, u32[]{:S(2)}) copy-start(f32[8192,128]{1,0:T(8,128)S(1)} %convolution_add_fusion) | copy-start | bytes 12582916
  383.0 9.7 %copy-start.12 = (f32[8192,64]{0,1:T(8,128)}, f32[8192,64]{0,1:T(8,128)S(1)}, u32[]{:S(2)}) copy-start(f32[8192,64]{0,1:T(8,128)S(1)} %convolution_add_fusion.3) | copy-start | bytes 6291460
  387.8 4.9 copy-start.26
  401.4 41.5 %copy-start.56 = (f32[8192,128]{1,0:T(8,128)}, f32[8192,128]{1,0:T(8,128)S(1)}, u32[]{:S(2)}) copy-start(f32[8192,128]{1,0:T(8,128)S(1)} %get-tuple-element.122) | copy-start | bytes 12582916
  494.6 7.3 copy-start.2
  494.6 10.1 %slice-start = ((s8[8388608]{0:T(1024)(128)(4,1)}), s8[4194304]{0:T(1024)(128)(4,1)S(1)}, s32[]{:S(2)}) async-start(s8[8388608]{0:T(1024)(128)(4,1)} %bitcast.299), calls=%async_computation.8 | async-start | bytes 8388608
  521.9 16.1 %copy-start.9 = (f32[6,8192]{1,0:T(8,128)S(1)}, f32[6,8192]{1,0:T(8,128)}, u32[]{:S(2)}) copy-start(f32[6,8192]{1,0:T(8,128)} %copy-done.8) | copy-start | bytes 589828
  521.9 16.1 %copy-start.11 = (f32[6,8192]{1,0:T(8,128)S(1)}, f32[6,8192]{1,0:T(8,128)}, u32[]{:S(2)}) copy-start(f32[6,8192]{1,0:T(8,128)} %copy-done.10) | copy-start | bytes 589828
  521.9 16.1 %copy-start.33 = (f32[6,128]{1,0:T(8,128)S(1)}, f32[6,128]{1,0:T(8,128)}, u32[]{:S(2)}) copy-start(f32[6,128]{1,0:T(8,128)} %param.21) | copy-start | bytes 9220
  521.9 16.1 %copy-start.40 = (f32[6,128]{1,0:T(8,128)S(1)}, f32[6,128]{1,0:T(8,128)}, u32[]{:S(2)}) copy-start(f32[6,128]{1,0:T(8,128)} %param.22) | copy-start | bytes 9220
  521.9 16.1 %copy-start.45 = (f32[6,128]{1,0:T(8,128)S(1)}, f32[6,128]{1,0:T(8,128)}, u32[]{:S(2)}) copy-start(f32[6,128]{1,0:T(8,128)} %param.23) | copy-start | bytes 9220
  570.4 6.1 copy-start.34
  570.4 196.0 %all-reduce.9.cloned.1.call-start = ((), (), s32[]{:S(2)}) async-start(), calls=%async_computation.5 | async-start | bytes 5373952 | tf_op jit(solution)/shard_map/psum | solution.py:202
  591.5 24.5 %copy-start.38 = (f32[512]{0:T(512)S(1)}, f32[512]{0:T(512)}, u32[]{:S(2)}) copy-start(f32[512]{0:T(512)} %copy-done.37) | copy-start | bytes 6148
  591.5 24.5 %copy-start.43 = (f32[512]{0:T(512)S(1)}, f32[512]{0:T(512)}, u32[]{:S(2)}) copy-start(f32[512]{0:T(512)} %copy-done.42) | copy-start | bytes 6148
  611.5 4.6 copy-start.3
  616.1 10.3 %copy-start.7 = (bf16[6,512,128]{2,1,0:T(8,128)(2,1)S(1)}, bf16[6,512,128]{2,1,0:T(8,128)(2,1)}, u32[]{:S(2)}) copy-start(bf16[6,512,128]{2,1,0:T(8,128)(2,1)} %copy-done.6) | copy-start | bytes 2359300
  626.3 159.4 %reduce-scatter.5.cloned.1.call-start = ((), (), s32[]{:S(2)}) async-start(), calls=%async_computation.4 | async-start | bytes 12582912 | tf_op jit(solution)/shard_map/reduce_scatter | solution.py:175
  653.9 6.5 slice-start.8
  655.8 4.5 copy-start.52
  655.9 4.5 slice-start.9
  664.6 25.7 %slice-start.2 = ((s8[25165824]{0:T(1024)(128)(4,1)}), s8[4194304]{0:T(1024)(128)(4,1)S(1)}, s32[]{:S(2)}) async-start(s8[25165824]{0:T(1024)(128)(4,1)} %bitcast.305), calls=%async_computation.10 | async-start | bytes 8388608
  664.6 25.7 %slice-start.3 = ((s8[25165824]{0:T(1024)(128)(4,1)}), s8[4194304]{0:T(1024)(128)(4,1)S(1)}, s32[]{:S(2)}) async-start(s8[25165824]{0:T(1024)(128)(4,1)} %bitcast.305), calls=%async_computation.11 | async-start | bytes 8388608
  669.1 21.3 %slice-start.4 = ((s8[25165824]{0:T(1024)(128)(4,1)}), s8[4194304]{0:T(1024)(128)(4,1)S(1)}, s32[]{:S(2)}) async-start(s8[25165824]{0:T(1024)(128)(4,1)} %bitcast.305), calls=%async_computation.12 | async-start | bytes 8388608
  669.1 21.3 %slice-start.5 = ((s8[25165824]{0:T(1024)(128)(4,1)}), s8[4194304]{0:T(1024)(128)(4,1)S(1)}, s32[]{:S(2)}) async-start(s8[25165824]{0:T(1024)(128)(4,1)} %bitcast.305), calls=%async_computation.13 | async-start | bytes 8388608
  679.4 10.2 %copy-start.28 = (f32[8192]{0:T(1024)S(1)}, f32[8192]{0:T(1024)}, u32[]{:S(2)}) copy-start(f32[8192]{0:T(1024)} %get-tuple-element.78) | copy-start | bytes 98308
  679.4 10.2 %copy-start.29 = (f32[8192]{0:T(1024)S(1)}, f32[8192]{0:T(1024)}, u32[]{:S(2)}) copy-start(f32[8192]{0:T(1024)} %get-tuple-element.106) | copy-start | bytes 98308
  679.4 10.9 %slice-start.6 = ((s8[25165824]{0:T(1024)(128)(4,1)}), s8[4194304]{0:T(1024)(128)(4,1)S(1)}, s32[]{:S(2)}) async-start(s8[25165824]{0:T(1024)(128)(4,1)} %bitcast.305), calls=%async_computation.14 | async-start | bytes 8388608
  679.4 11.0 %slice-start.7 = ((s8[25165824]{0:T(1024)(128)(4,1)}), s8[4194304]{0:T(1024)(128)(4,1)S(1)}, s32[]{:S(2)}) async-start(s8[25165824]{0:T(1024)(128)(4,1)} %bitcast.305), calls=%async_computation.15 | async-start | bytes 8388608
  777.4 111.8 %copy-start.25 = (f32[8192]{0:T(1024)S(1)}, f32[8192]{0:T(1024)}, u32[]{:S(2)}) copy-start(f32[8192]{0:T(1024)} %get-tuple-element.103) | copy-start | bytes 98308
  889.2 10.1 %copy-start.1 = (f32[6,256]{1,0:T(8,128)S(1)}, f32[6,256]{1,0:T(8,128)}, u32[]{:S(2)}) copy-start(f32[6,256]{1,0:T(8,128)} %param.25) | copy-start | bytes 18436
  (26 other events, 69.3 us)
Sparse Core Ops, SparseCore 0:
  129.0 16.5 all-reduce.12
  186.9 64.5 reduce-scatter.2
  264.7 41.4 all-gather.1
  570.5 19.9 all-reduce.10
  626.4 139.9 all-reduce.8
  769.2 16.4 reduce-scatter.4
where the time goes:
time: 916 us; the launch traced here: 906 us
  matrix products  312 us (34%)
  other arithmetic  209 us (23%)
  waiting for transfers between devices  199 us (22%)
  blocking collectives  158 us (17%)
  between operations  15.2 us (2%)
  local copies, waits for them, and re-layouts  12.7 us (1%)
    psum x1, blocking collectives, on_device(): lax.psum((jnp.sum(normed_gradient_local, axis=0), jnp.sum(normed_gradient...  77.2 us
    reduce_scatter x1, waiting for transfers between devices, on_device(): lax.psum_scatter(partial_out, 'mp', scatter_dimension=2, tiled=True)  64.6 us
    psum x1, waiting for transfers between devices, on_device(): summed_all = lax.psum(expert_terms + head_terms, 'batch')  63 us
    dot_general x2, matrix products, on_device(): grad_first.append(jnp.dot(mixed.T, d_first, precision=HIGHEST))  48.3 us
    psum x1, blocking collectives, on_device(): lax.psum((jnp.sum(weight_matrix[:, None] * features_f, axis=0), jnp.sum(w...  44.2 us
    dot_general x2, matrix products, on_device(): jnp.dot(mixed, tower_first[task_id], precision=HIGHEST)  36.9 us
    psum x1, blocking collectives, on_device(): lax.psum(jnp.sum(weight_matrix[:, None] * mean_removed * mean_removed, ax...  36.6 us
    dot_general x2, matrix products, on_device(): d_mixed = jnp.dot(d_first, tower_first[task_id].T, precision=HIGHEST)  36.4 us
  transfers between devices with their start and end apart: 6, of which 6 were waited for; matrix products, arithmetic and copies ran while one was open for 11% of the time, Pallas kernels for 0%

commit v1 on v0

v1 whole, which is shorter than its diff:
```python
import functools

import jax
import jax.numpy as jnp
from jax import lax
from jax.experimental import pallas as pl
from jax.experimental.pallas import tpu as pltpu
from jax.sharding import PartitionSpec as P

MESH = pl.DeviceIdType.MESH
F32 = jnp.float32
BF16 = jnp.bfloat16
EPS = 1e-05
TASK_EXPERTS = ((0, 1, 4, 5), (2, 3, 4, 5))
E = 6
H = 256
D = 512
TF = 256
TB = 512
SB = 256
CH = 32
VR = 72
CW = 384
NC = E + 1


def levels_of(count):
    levels, stride = [], 1
    while stride < count:
        radix = 4 if (count // stride) % 4 == 0 else count // stride
        levels.append((stride, radix))
        stride *= radix
    return levels


def plan_of(count):
    plan, rows = [], H
    for stride, radix in levels_of(count):
        split = rows % radix == 0 and (rows // radix) % 16 == 0
        plan.append((stride, radix, rows, rows // radix if split else rows))
        rows = plan[-1][3]
    return plan


def nn(a, b):
    return lax.dot_general(a, b, (((1,), (0,)), ((), ())), preferred_element_type=F32)


def nt(a, b):
    return lax.dot_general(a, b, (((1,), (1,)), ((), ())), preferred_element_type=F32)


def column(row):
    return jnp.broadcast_to(row, (128, 128)).T


def wide(table, width):
    return jnp.concatenate([table] * (width // 128), axis=1)


def fold8(value):
    total = value[0:8]
    for start in range(8, value.shape[0], 8):
        total = total + value[start : start + 8]
    return total


def fold_lanes(value):
    total = value[:, 0:128]
    for start in range(128, value.shape[1], 128):
        total = total + value[:, start : start + 128]
    return total


def lane_sums(partial):
    ones = jnp.ones((8, 128), F32)
    sums = lax.dot_general(
        ones, partial, (((1,), (1,)), ((), ())),
        preferred_element_type=F32, precision=lax.Precision.HIGHEST,
    )
    return sums[0:1]


def merge_stats(items):
    count = items[0][2:3]
    total = items[0][0:1]
    for item in items[1:]:
        count = count + item[2:3]
        total = total + item[0:1]
    mean = total / jnp.maximum(count, 1.0)
    square = jnp.zeros_like(total)
    for item in items:
        shift = item[0:1] / jnp.maximum(item[2:3], 1.0) - mean
        square = square + item[1:2] + item[2:3] * shift * shift
    return total, square, count


def main_kernel(
    plan, rows_core,
    x_hbm, v_ref, y_ref, win_ref, wout_ref, bin_ref, gain_ref, nb_ref, bout_ref, gate_ref, gb_ref,
    w1_ref, b1_ref, w2_ref, b2_ref, wl_ref, bl_ref,
    d_hbm, pred_hbm, gout_hbm, vout_ref, stat_ref,
    xbuf, zbuf, hbuf, dobuf, rbuf, dlogbuf, predbuf,
    wf, wb, gback, wot, wo, bct, g2t, b2t, gt, bot,
    w1t, w1n, w2f, w2b, b1t, b2tt, wlt, gbt,
    abuf, obuf, mixb, u1b, dmix,
    acc_in, acc_out, acc_gate, acc_first, acc_second,
    acc_u, acc_dlog, acc_lb, acc_last, acc_b2, acc_b1, s2row, vec,
    bias_snd, bias_rcv,
    st_mp, st_lv, v_mp, v_lv, hkeep, mprecv, lvrecv,
    sem_x, sem_w, sem_st, sem_v, sem_s, sem_r, sem_l, sem_d,
):
    R = rows_core
    n_levels = len(plan)
    b = lax.axis_index("batch")
    mp = lax.axis_index("mp")
    other = 1 - mp
    digits = [lax.rem(lax.div(b, stride), radix) for stride, radix, _, _ in plan]

    def peer(level, step):
        stride, radix = plan[level][:2]
        to = lax.rem(digits[level] + step, radix)
        return (b + (to - digits[level]) * stride, mp)

    def send(src, dst, ssem, rsem, to):
        copy = pltpu.make_async_remote_copy(
            src_ref=src, dst_ref=dst, send_sem=ssem, recv_sem=rsem,
            device_id=to, device_id_type=MESH,
        )
        copy.start()
        return copy

    n_x = 8
    xr = R // n_x
    x_copies = []
    for k in range(n_x):
        copy = pltpu.make_async_copy(
            x_hbm.at[pl.ds(pl.multiple_of(mp * R + k * xr, 16), xr), :],
            xbuf.at[pl.ds(k * xr, xr), :],
            sem_x.at[k],
        )
        copy.start()
        x_copies.append(copy)

    barrier = pltpu.get_barrier_semaphore()
    greets = [(b, other)]
    for level in range(n_levels):
        greets += [peer(level, step) for step in range(1, plan[level][1])]
    for to in greets:
        pl.semaphore_signal(barrier, inc=1, device_id=to, device_id_type=MESH)
    pl.semaphore_wait(barrier, len(greets))

    win_snd = dobuf.at[0:D, 0 : E * 128]
    win_rcv = dobuf.at[0:D, 1024 : 1024 + E * 128]
    wout_snd = dobuf.at[D : D + 128, 0 : E * H]
    wout_rcv = dobuf.at[D : D + 128, 2048 : 2048 + E * H]
    for e in range(E):
        win_snd[:, e * 128 : (e + 1) * 128] = win_ref[e].astype(BF16)
        wout_snd[:, e * H : (e + 1) * H] = wout_ref[e].astype(BF16)
    bias_snd[0:E] = bin_ref[...]
    bias_snd[8 : 8 + E] = gain_ref[...]
    bias_snd[16 : 16 + E] = nb_ref[...]
    w_copies = [
        send(win_snd, win_rcv, sem_w.at[0], sem_w.at[1], (b, other)),
        send(wout_snd, wout_rcv, sem_w.at[2], sem_w.at[3], (b, other)),
        send(bias_snd, bias_rcv, sem_w.at[4], sem_w.at[5], (b, other)),
    ]

    v_row = v_ref[:, pl.ds(pl.multiple_of(mp * R, 128), R)].astype(F32)
    count = jnp.sum(v_row, axis=1, keepdims=True)
    total = jnp.zeros((16, D), F32)
    for k in range(n_x):
        x_copies[k].wait()
        v16 = jnp.broadcast_to(v_row[:, k * xr : (k + 1) * xr], (16, xr)).astype(BF16)
        total = total + nn(v16, xbuf[pl.ds(k * xr, xr), :])
    mean = total[0:1] / jnp.maximum(count, 1.0)

    def square_step(k, total):
        r0 = pl.multiple_of(k * 256, 256)
        off = xbuf[pl.ds(r0, 256), :].astype(F32) - mean
        v16 = v_ref[:, pl.ds(pl.multiple_of(mp * R + k * 256, 128), 256)]
        v16 = jnp.broadcast_to(v16.astype(F32), (16, 256)).astype(BF16)
        return total + nn(v16, (off * off).astype(BF16))

    square = lax.fori_loop(0, R // 256, square_step, jnp.zeros((16, D), F32))
    st_mp[mp] = jnp.concatenate(
        [total[0:1], square[0:1], jnp.broadcast_to(count, (1, D)), jnp.zeros((5, D), F32)], axis=0
    )
    st_copy = send(st_mp.at[mp], st_mp.at[mp], sem_st.at[0], sem_st.at[1], (b, other))

    for t in range(2):
        w1n[t] = w1_ref[t].astype(BF16)
        w1t[t] = w1_ref[t].T.astype(BF16)
        b1t[t * 128 : (t + 1) * 128] = column(b1_ref[t : t + 1, :])
        for k in range(2):
            for e in range(3 * t, 3 * t + 3):
                bot[e * H + k * 128 : e * H + (k + 1) * 128] = column(
                    bout_ref[e : e + 1, k * 128 : (k + 1) * 128]
                )
    zero64 = jnp.zeros((64, 128), F32)
    zero128 = jnp.zeros((128, 64), F32)
    w2f[0:64] = jnp.concatenate([w2_ref[0], zero64], axis=1).astype(BF16)
    w2f[64:128] = jnp.concatenate([zero64, w2_ref[1]], axis=1).astype(BF16)
    w2b[0:128] = jnp.concatenate([w2_ref[0].T, zero128], axis=1).astype(BF16)
    w2b[128:256] = jnp.concatenate([zero128, w2_ref[1].T], axis=1).astype(BF16)
    b2tt[...] = column(jnp.concatenate([b2_ref[0:1, :], b2_ref[1:2, :]], axis=1))
    wlt[...] = column(jnp.concatenate([wl_ref[0:1, :], wl_ref[1:2, :]], axis=1))
    gbt[...] = jnp.concatenate(
        [jnp.full((1, 128), gb_ref[t, k], F32) for t in range(2) for k in range(4)], axis=0
    )
    gate = jnp.concatenate([gate_ref[0], gate_ref[1]], axis=0)
    gate_low = gate.astype(BF16).astype(F32)
    gback[...] = jnp.concatenate([gate_low, gate_low, jnp.zeros((112, D), F32)], axis=0).T.astype(BF16)
    acc_gate[...] = jnp.zeros_like(acc_gate)
    acc_first[...] = jnp.zeros_like(acc_first)
    acc_second[...] = jnp.zeros_like(acc_second)
    acc_dlog[...] = jnp.zeros_like(acc_dlog)
    acc_lb[...] = jnp.zeros_like(acc_lb)
    acc_last[...] = jnp.zeros_like(acc_last)
    acc_b1[...] = jnp.zeros_like(acc_b1)
    acc_b2[...] = jnp.zeros_like(acc_b2)

    def place(half, win, wout, bias):
        for e in range(E):
            at = pl.multiple_of(e * H + half * 128, 128)
            w = win[:, e * 128 : (e + 1) * 128]
            wb[:, pl.ds(at, 128)] = w
            wf[pl.ds(at, 128), :] = w.T
            o = wout[:, e * H : (e + 1) * H]
            wo[pl.ds(at, 128), :] = (o.astype(F32) * 0.5).astype(BF16)
            wot[pl.ds(e * H, H), pl.ds(pl.multiple_of(half * 128, 128), 128)] = o.T
            bct[pl.ds(at, 128), :] = column(bias[e : e + 1, :])
            gain = column(bias[8 + e : 9 + e, :])
            gt[pl.ds(at, 128), :] = gain
            g2t[pl.ds(at, 128), :] = gain * 0.5
            b2t[pl.ds(at, 128), :] = column(bias[16 + e : 17 + e, :]) * 0.5

    place(mp, win_snd, wout_snd, bias_snd)
    st_copy.wait()
    total, square, count = merge_stats([st_mp[0], st_mp[1]])
    st_copies = []
    for level in range(n_levels):
        own = digits[level]
        st_lv[level, own] = jnp.concatenate([total, square, count, jnp.zeros((5, D), F32)], axis=0)
        copies = []
        for step in range(1, plan[level][1]):
            base = 2 + (level * 3 + step - 1) * 2
            copies.append(
                send(
                    st_lv.at[level, own], st_lv.at[level, own],
                    sem_st.at[base], sem_st.at[base + 1], peer(level, step),
                )
            )
        if level == 0:
            for copy in w_copies:
                copy.wait()
            place(other, win_rcv, wout_rcv, bias_rcv)
            means = []
            for e in range(E):
                w = wf[e * H : (e + 1) * H, :].astype(F32)
                means.append(jnp.sum(w, axis=0, keepdims=True) * (1.0 / H))
                shift = jnp.sum(bct[e * H : (e + 1) * H, :], axis=0, keepdims=True) * (1.0 / H)
                bct[e * H : (e + 1) * H, :] = bct[e * H : (e + 1) * H, :] - shift
            pad = [jnp.zeros((2, D), F32)]
            means = jnp.concatenate(means + pad, axis=0)
            means_high = means.astype(BF16).astype(F32)
            wf[E * H : E * H + 32, :] = jnp.concatenate(
                [gate_low, means_high, means - means_high, jnp.zeros((8, D), F32)], axis=0
            ).astype(BF16)
        for copy in copies:
            copy.wait()
        total, square, count = merge_stats([st_lv[level, k] for k in range(plan[level][1])])
    mu = total / count
    inv = lax.rsqrt(square / count + EPS)
    stat_ref[...] = jnp.concatenate([mu, inv, count, jnp.zeros((5, D), F32)], axis=0)

    def forward(i):
        r0 = pl.multiple_of(i * TF, TF)
        x_tile = xbuf[pl.ds(r0, TF), :].astype(F32)
        xn = ((x_tile - stat_ref[0:1, :]) * stat_ref[1:2, :]).astype(BF16)
        xbuf[pl.ds(r0, TF), :] = xn
        ext = nt(wf[E * H : E * H + 32, :], xn)
        for e in range(E):
            abuf[e * H : (e + 1) * H, :] = nt(wf[e * H : (e + 1) * H, :], xn)
        for e in range(E):
            mean = ext[8 + e : 9 + e] + ext[16 + e : 17 + e]
            squares = jnp.zeros((8, TF), F32)
            for at in range(e * H, (e + 1) * H, CH):
                c = (abuf[at : at + CH, :] - mean) + wide(bct[at : at + CH, :], TF)
                abuf[at : at + CH, :] = c
                squares = squares + fold8(c * c)
            r = lax.rsqrt(jnp.sum(squares, axis=0, keepdims=True) * (1.0 / H) + EPS)
            rbuf[e : e + 1, pl.ds(r0, TF)] = r
            for at in range(e * H, (e + 1) * H, CH):
                zhat = abuf[at : at + CH, :] * r
                zbuf[at : at + CH, pl.ds(r0, TF)] = zhat.astype(BF16)
                half = zhat * wide(g2t[at : at + CH, :], TF) + wide(b2t[at : at + CH, :], TF)
                hbuf[at : at + CH, pl.ds(r0, TF)] = (half * (1.0 + jnp.tanh(half))).astype(BF16)
            o = nn(wot[e * H : (e + 1) * H, :], hbuf[e * H : (e + 1) * H, pl.ds(r0, TF)])
            obuf[e * H : (e + 1) * H, :] = o + wide(bot[e * H : (e + 1) * H, :], TF)
        return ext

    def heads(i, ext):
        r0 = pl.multiple_of(i * TF, TF)
        v0 = pl.multiple_of(mp * R + i * TF, 128)
        logits = ext[0:8] + wide(gbt[...], TF)
        probs = []
        for t in range(2):
            part = logits[4 * t : 4 * t + 4]
            part = jnp.exp(part - jnp.max(part, axis=0, keepdims=True))
            part = part / jnp.sum(part, axis=0, keepdims=True)
            probs.append([part[k : k + 1] for k in range(4)])
        for at in range(0, H, CH):
            for t in range(2):
                mixed = None
                for k in range(4):
                    e = TASK_EXPERTS[t][k]
                    term = probs[t][k] * obuf[e * H + at : e * H + at + CH, :]
                    mixed = term if mixed is None else mixed + term
                mixb[t * H + at : t * H + at + CH, :] = mixed.astype(BF16)
        slopes = []
        for t in range(2):
            pre = nn(w1t[t], mixb[t * H : (t + 1) * H, :])
            half = (pre + wide(b1t[t * 128 : (t + 1) * 128, :], TF)) * 0.5
            p = 1.0 + jnp.tanh(half)
            u1b[t * 128 : (t + 1) * 128, :] = (half * p).astype(BF16)
            slopes.append(0.5 * p * (1.0 + half * (2.0 - p)))
        half = (nn(w2f[...], u1b[...]) + wide(b2tt[...], TF)) * 0.5
        p = 1.0 + jnp.tanh(half)
        u2 = half * p
        slope2 = 0.5 * p * (1.0 + half * (2.0 - p))
        wl = wide(wlt[...], TF)
        weighted = u2 * wl
        d_logits = []
        valid = v_ref[:, pl.ds(v0, TF)].astype(F32)
        for t in range(2):
            logit = jnp.sum(weighted[t * 64 : (t + 1) * 64], axis=0, keepdims=True) + bl_ref[t]
            pred = 0.5 + 0.5 * jnp.tanh(0.5 * logit)
            predbuf[t : t + 1, pl.ds(r0, TF)] = pred
            label = y_ref[t : t + 1, pl.ds(v0, TF)].astype(F32)
            d_logits.append(valid * (pred - label))
        d_logit = jnp.concatenate(
            [jnp.broadcast_to(d_logits[t], (64, TF)) for t in range(2)], axis=0
        )
        acc_last[...] += fold_lanes(u2 * d_logit)
        acc_lb[0:2] += fold_lanes(jnp.concatenate(d_logits, axis=0))
        d2 = d_logit * wl * slope2
        acc_b2[...] += fold_lanes(d2)
        d2_low = d2.astype(BF16)
        acc_second[...] += nt(d2_low, u1b[...])
        d_u1 = nn(w2b[...], d2_low)
        for t in range(2):
            d1 = d_u1[t * 128 : (t + 1) * 128] * slopes[t]
            acc_b1[t * 128 : (t + 1) * 128] += fold_lanes(d1)
            d1_low = d1.astype(BF16)
            acc_first[t] += nt(mixb[t * H : (t + 1) * H, :], d1_low)
            dmix[t * H : (t + 1) * H, :] = nn(w1n[t], d1_low)
        dots = [[jnp.zeros((8, TF), F32) for _ in range(4)] for _ in range(2)]
        for at in range(0, H, CH):
            dm = [dmix[t * H + at : t * H + at + CH, :] for t in range(2)]
            grads = [None] * E
            for t in range(2):
                for k in range(4):
                    e = TASK_EXPERTS[t][k]
                    term = probs[t][k] * dm[t]
                    grads[e] = term if grads[e] is None else grads[e] + term
                    o = obuf[e * H + at : e * H + at + CH, :]
                    dots[t][k] = dots[t][k] + fold8(dm[t] * o)
            for e in range(E):
                dobuf[e * H + at : e * H + at + CH, pl.ds(r0, TF)] = grads[e].astype(BF16)
        rows = []
        for t in range(2):
            sums = [jnp.sum(dots[t][k], axis=0, keepdims=True) for k in range(4)]
            centre = sum(probs[t][k] * sums[k] for k in range(4))
            rows += [probs[t][k] * (sums[k] - centre) for k in range(4)]
        d_gate = jnp.concatenate(rows, axis=0)
        acc_dlog[...] += fold_lanes(d_gate)
        high = d_gate.astype(BF16).astype(F32)
        d_gate = jnp.concatenate([high, d_gate - high], axis=0).astype(BF16)
        dlogbuf[:, pl.ds(r0, TF)] = d_gate
        acc_gate[...] += nn(d_gate, xbuf[pl.ds(r0, TF), :])

    def forward_step(i, carry):
        heads(i, forward(i))
        return carry

    lax.fori_loop(0, R // TF, forward_step, 0)

    pending = []
    pred_at = pl.ds(pl.multiple_of(mp * R, 128), R)
    pred_local = pltpu.make_async_copy(predbuf, pred_hbm.at[:, pred_at], sem_l.at[0])
    pred_local.start()
    pending.append(pred_local)
    pending.append(send(predbuf, pred_hbm.at[:, pred_at], sem_w.at[6], sem_w.at[7], (b, other)))

    flight = {}
    n_sems = 1 + 2 * sum(radix - 1 for _, radix, _, _ in plan)

    def source(c, rows, place_at):
        base = 2048 if c == E else 0
        e = 0 if c == E else c
        return hbuf.at[pl.ds(e * H, rows), pl.ds(base + place_at * CW, CW)]

    def level_sems(level):
        return 1 + 2 * sum(radix - 1 for _, radix, _, _ in plan[:level])

    def start_pair(c):
        src = source(c, H, 0)
        flight[c] = [send(src, mprecv.at[c], sem_s.at[c, 0], sem_r.at[c, 0], (b, other))]

    def start_level(c, level, value):
        stride, radix, rows, after = plan[level]
        out = source(c, rows, 1 + level)
        out[...] = value.astype(BF16)
        copies = []
        for step in range(1, radix):
            k = level_sems(level) + step - 1
            part = out
            if after != rows:
                to = lax.rem(digits[level] + step, radix)
                part = out.at[pl.ds(pl.multiple_of(to * after, 16), after), :]
            dst = lvrecv[level].at[c, step]
            copies.append(send(part, dst, sem_s.at[c, k], sem_r.at[c, k], peer(level, step)))
        flight[c] = copies
        if after != rows:
            mine = out[pl.ds(pl.multiple_of(digits[level] * after, 16), after), :]
        else:
            mine = out[...]
        lvrecv[level][c, 0] = mine

    def finish_level(c, level):
        stride, radix, rows, after = plan[level]
        for copy in flight[c]:
            copy.wait()
        if after != rows:
            parts = [lvrecv[level][c, step].astype(F32) for step in range(radix)]
            return functools.reduce(lambda p, q: p + q, parts)
        total = None
        for k in range(radix):
            step = lax.rem(k - digits[level] + radix, radix)
            part = lvrecv[level][c, step].astype(F32)
            total = part if total is None else total + part
        return total

    def region(c, level):
        at = 0
        for k in range(level + 1):
            if plan[k][2] != plan[k][3]:
                at = at + digits[k] * plan[k][3]
        rows = plan[level][3] if level >= 0 else H
        if isinstance(at, int):
            return gout_hbm.at[c, pl.ds(at, rows), :]
        return gout_hbm.at[c, pl.ds(pl.multiple_of(at, 16), rows), :]

    split = [level for level in range(n_levels) if plan[level][2] != plan[level][3]]

    def start_result(c, value):
        rows = plan[-1][3]
        final = source(c, rows, 1 + n_levels)
        final[...] = value.astype(BF16)
        local = pltpu.make_async_copy(final, region(c, n_levels - 1), sem_l.at[1 + c])
        local.start()
        flight[c] = [local]
        if split:
            start_gather(c, split[-1], final)

    def start_gather(c, level, src):
        dst = region(c, level)
        for step in range(1, plan[level][1]):
            k = level_sems(level) + plan[level][1] - 1 + step - 1
            flight[c].append(send(src, dst, sem_s.at[c, k], sem_r.at[c, k], peer(level, step)))

    def chunk_steps(c):
        steps = []

        def from_pair():
            for copy in flight[c]:
                copy.wait()
            if c < E:
                value = hkeep[c % 2] + mprecv[c].astype(F32)
            else:
                value = source(c, H, 0)[...].astype(F32) + mprecv[c].astype(F32)
            start_level(c, 0, value)

        steps.append(from_pair)
        for level in range(n_levels):

            def next_level(level=level):
                value = finish_level(c, level)
                if level + 1 < n_levels:
                    start_level(c, level + 1, value)
                else:
                    start_result(c, value)

            steps.append(next_level)
        for place_in in range(len(split) - 1, 0, -1):

            def gather(place_in=place_in):
                for copy in flight[c]:
                    copy.wait()
                flight[c] = []
                start_gather(c, split[place_in - 1], region(c, split[place_in] - 1))

            steps.append(gather)

        def finish():
            for copy in flight[c]:
                copy.wait()
            flight[c] = []

        steps.append(finish)
        return steps

    queue = []

    def turn():
        for steps in list(queue):
            steps.pop(0)()
            if not steps:
                queue.remove(steps)

    def pack_towers():
        src = source(E, H, 0)
        src[:, 0:128] = acc_first[0].astype(BF16)
        src[:, 128:256] = acc_first[1].astype(BF16)
        gates = acc_gate[0:8] + acc_gate[8:16]
        rest = [acc_second[0:64, 0:128], acc_second[64:128, 128:256]]
        rest += [gates[:, k * 128 : (k + 1) * 128] for k in range(4)]
        rest.append(jnp.zeros((H - 160, 128), F32))
        src[:, 256:384] = jnp.concatenate(rest, axis=0).astype(BF16)

    def pack_expert(e):
        def half(h):
            at = pl.ds(pl.multiple_of(h * 128, 128), 128)
            a, o = acc_in[at, :], acc_out[at, :]
            top = jnp.concatenate([a[:, 0:256], o[:, 0:128]], axis=1)
            low = jnp.concatenate([a[:, 256:512], o[:, 128:256]], axis=1)
            return top, low

        top, low = half(mp)
        hkeep[e % 2, 0:128] = top
        hkeep[e % 2, 128:256] = low
        src = source(e, H, 0)
        top, low = half(other)
        src[0:128, :] = top.astype(BF16)
        src[128:256, :] = low.astype(BF16)

    ones16 = jnp.ones((16, SB), BF16)
    s2row[...] = jnp.sum(
        (gate_low * (acc_gate[0:8] + acc_gate[8:16])), axis=0, keepdims=True
    )

    def backward_part(e, r0):
        at0 = e * H
        lanes = pl.ds(r0, SB)
        do = dobuf[at0 : at0 + H, lanes]
        dmix[0:H, :] = nn(wo[at0 : at0 + H, :], do)
        acc_out[...] += nt(hbuf[at0 : at0 + H, lanes], do)
        vec[3] += nt(ones16, do)[0:8]
        r = rbuf[e : e + 1, lanes]
        m1 = jnp.zeros((8, SB), F32)
        m2 = jnp.zeros((8, SB), F32)
        for u in range(0, H, CH):
            at = at0 + u
            zhat = zbuf[at : at + CH, lanes].astype(F32)
            half = zhat * wide(g2t[at : at + CH, :], SB) + wide(b2t[at : at + CH, :], SB)
            p = 1.0 + jnp.tanh(half)
            dz = dmix[u : u + CH, :] * (p * (1.0 + half * (2.0 - p)))
            q = dz * zhat
            acc_u[0, u : u + CH, :] += fold_lanes(dz)
            acc_u[1, u : u + CH, :] += fold_lanes(q)
            g = wide(gt[at : at + CH, :], SB)
            dzg = dz * g
            dmix[u : u + CH, :] = dzg
            m1 = m1 + fold8(dzg)
            m2 = m2 + fold8(q * g)
        m1 = jnp.sum(m1, axis=0, keepdims=True) * (1.0 / H)
        m2 = jnp.sum(m2, axis=0, keepdims=True) * (1.0 / H)
        for u in range(0, H, CH):
            at = at0 + u
            zhat = zbuf[at : at + CH, lanes].astype(F32)
            da = r * (dmix[u : u + CH, :] - m1 - zhat * m2)
            acc_u[2, u : u + CH, :] += fold_lanes(da)
            zbuf[at : at + CH, lanes] = da.astype(BF16)
        acc_in[...] += nn(zbuf[at0 : at0 + H, lanes], xbuf[pl.ds(r0, SB), :])

    for e in range(E):
        acc_in[...] = jnp.zeros_like(acc_in)
        acc_out[...] = jnp.zeros_like(acc_out)
        acc_u[...] = jnp.zeros_like(acc_u)
        vec[3] = jnp.zeros((8, H), F32)

        def backward_step(i, carry, e=e):
            for part in range(TB // SB):
                backward_part(e, pl.multiple_of(i * TB + part * SB, SB))
            return carry

        n_b = R // TB
        lax.fori_loop(0, n_b // 2, backward_step, 0)
        turn()
        lax.fori_loop(n_b // 2, n_b, backward_step, 0)
        turn()
        if e == 0:
            pack_towers()
            start_pair(E)
            queue.append(chunk_steps(E))
        pack_expert(e)
        start_pair(e)
        queue.append(chunk_steps(e))
        for k, row in ((0, 2), (1, 1), (2, 0)):
            sums = lane_sums(acc_u[row])
            v_mp[mp, k * 12 + 2 * e : k * 12 + 2 * e + 1, :] = sums[:, 0:128]
            v_mp[mp, k * 12 + 2 * e + 1 : k * 12 + 2 * e + 2, :] = sums[:, 128:256]
        bo = vec[3][0:1]
        v_mp[mp, 36 + 2 * e : 37 + 2 * e, :] = bo[:, 0:128]
        v_mp[mp, 37 + 2 * e : 38 + 2 * e, :] = bo[:, 128:256]
        cross = jnp.zeros((8, D), F32)
        for u in range(0, H, CH):
            w = wf[e * H + u : e * H + u + CH, :].astype(F32)
            cross = cross + fold8(w * acc_in[u : u + CH, :])
        s2row[...] += jnp.sum(cross, axis=0, keepdims=True)

    for k in range(4):
        v_mp[mp, 48 + k : 49 + k, :] = s2row[:, k * 128 : (k + 1) * 128]
    v_mp[mp, 52:60, :] = acc_dlog[...]
    v_mp[mp, 60:61, :] = lane_sums(acc_last[...])
    v_mp[mp, 61:63, :] = acc_lb[0:2]
    b1_sums = lane_sums(acc_b1[...])
    v_mp[mp, 63:64, :] = b1_sums[:, 0:128]
    v_mp[mp, 64:65, :] = b1_sums[:, 128:256]
    v_mp[mp, 65:66, :] = lane_sums(acc_b2[...])
    v_mp[mp, 66:VR, :] = jnp.zeros((VR - 66, 128), F32)
    flight["v"] = [send(v_mp.at[mp], v_mp.at[mp], sem_v.at[0], sem_v.at[1], (b, other))]

    def small_level(level, total):
        own = digits[level]
        v_lv[level, own] = total
        flight["v"] = []
        for step in range(1, plan[level][1]):
            base = 2 + (level * 3 + step - 1) * 2
            flight["v"].append(
                send(
                    v_lv.at[level, own], v_lv.at[level, own],
                    sem_v.at[base], sem_v.at[base + 1], peer(level, step),
                )
            )

    def small_steps():
        steps = []

        def first():
            for copy in flight["v"]:
                copy.wait()
            small_level(0, v_mp[0] + v_mp[1])

        steps.append(first)
        for level in range(n_levels):

            def step(level=level):
                for copy in flight["v"]:
                    copy.wait()
                total = v_lv[level, 0]
                for k in range(1, plan[level][1]):
                    total = total + v_lv[level, k]
                if level + 1 < n_levels:
                    small_level(level + 1, total)
                    return
                vout_ref[...] = total
                row = jnp.concatenate([total[k : k + 1] for k in range(2 * E)], axis=1)
                row_high = row.astype(BF16).astype(F32)
                rows = jnp.concatenate(
                    [row_high, row - row_high, jnp.zeros((14, E * H), F32)], axis=0
                ).astype(BF16)
                s1 = nn(rows, wf[0 : E * H, :])
                gate_sum = jnp.sum(total[52:60], axis=1, keepdims=True)
                gate_part = jnp.sum(gate_low * gate_sum, axis=0, keepdims=True)
                stat_ref[3:4, :] = s1[0:1] + s1[1:2] + gate_part
                stat_ref[4:5, :] = jnp.concatenate([total[48 + k : 49 + k] for k in range(4)], axis=1)

            steps.append(step)
        return steps

    queue.append(small_steps())

    def input_gradient(i, carry):
        r0 = pl.multiple_of(i * TB, TB)
        lanes = pl.ds(r0, TB)
        da = zbuf[:, lanes]
        dl = dlogbuf[:, lanes]
        for k, half in ((0, mp), (1, other)):
            at = pl.ds(pl.multiple_of(half * 256, 256), 256)
            grad = nn(wb[at, :], da) + nn(gback[at, 0:16], dl)
            dobuf[k * H : (k + 1) * H, lanes] = grad.astype(BF16)
        return carry

    n_c = R // TB
    for part in range(4):
        lax.fori_loop(part * n_c // 4, (part + 1) * n_c // 4, input_gradient, 0)
        turn()
        w = R // 4
        at = pl.ds(part * w, w)
        to = pl.ds(pl.multiple_of(mp * R + part * w, 128), w)
        local = pltpu.make_async_copy(dobuf.at[0:H, at], d_hbm.at[:, to], sem_l.at[8 + part])
        local.start()
        pending.append(local)
        pending.append(
            send(dobuf.at[H : 2 * H, at], d_hbm.at[:, to], sem_d.at[part], sem_d.at[4 + part], (b, other))
        )
    while queue:
        turn()
    for copy in pending:
        copy.wait()


def final_kernel(
    rows_tile, dt_ref, x_ref, v_ref, pred_ref, gout_ref, vout_ref, stat_ref,
    o_pred, o_feat, o_in, o_inb, o_gain, o_nb, o_out, o_outb, o_gate, o_gateb,
    o_w1, o_b1, o_w2, o_b2, o_wl, o_bl,
):
    mp = lax.axis_index("mp")
    half = pl.ds(pl.multiple_of(mp * 256, 256), 256)
    count = stat_ref[2:3, half]
    inv = stat_ref[1:2, half]
    mu = stat_ref[0:1, half]
    s1 = stat_ref[3:4, half] / count
    s2 = stat_ref[4:5, half] / count
    for at in range(0, rows_tile, 128):
        valid = jnp.broadcast_to(v_ref[:, at : at + 128].astype(F32), (128, 128)).T
        for k in range(2):
            cols = slice(k * 128, (k + 1) * 128)
            grad = dt_ref[cols, at : at + 128].astype(F32).T
            xhat = (x_ref[at : at + 128, cols].astype(F32) - mu[:, cols]) * inv[:, cols]
            o_feat[at : at + 128, cols] = inv[:, cols] * (
                grad - valid * (s1[:, cols] + xhat * s2[:, cols])
            )

    @pl.when(pl.program_id(0) == 0)
    def _():
        scale = 1.0 / stat_ref[2:3, 0:128]
        o_pred[...] = pred_ref[...]
        for e in range(E):
            g = gout_ref[e].astype(F32) * scale[:, 0:1]
            for k in range(2):
                o_in[e, k * 256 : k * 256 + 128, :] = g[k * 128 : (k + 1) * 128, 0:128].T
                o_in[e, k * 256 + 128 : k * 256 + 256, :] = g[k * 128 : (k + 1) * 128, 128:256].T
                o_out[e, :, k * 128 : (k + 1) * 128] = g[k * 128 : (k + 1) * 128, 256:384]
            for ref, base in ((o_inb, 0), (o_gain, 12), (o_nb, 24)):
                ref[e : e + 1, :] = vout_ref[pl.ds(base + 2 * e + mp, 1), :] * scale
            for k in range(2):
                o_outb[e : e + 1, k * 128 : (k + 1) * 128] = (
                    vout_ref[36 + 2 * e + k : 37 + 2 * e + k, :] * scale
                )
        g = gout_ref[E].astype(F32) * scale[:, 0:1]
        o_w1[0] = g[:, 0:128]
        o_w1[1] = g[:, 128:256]
        o_w2[0] = g[0:64, 256:384]
        o_w2[1] = g[64:128, 256:384]
        for k in range(4):
            part = g[128 + 8 * k : 136 + 8 * k, 256:384]
            o_gate[0, :, k * 128 : (k + 1) * 128] = part[0:4]
            o_gate[1, :, k * 128 : (k + 1) * 128] = part[4:8]
        gate_bias = jnp.sum(vout_ref[52:60, :], axis=1, keepdims=True) * scale
        table = jnp.concatenate([gate_bias, jnp.zeros((120, 128), F32)], axis=0).T
        o_gateb[0:1, :] = table[0:1, 0:4]
        o_gateb[1:2, :] = table[0:1, 4:8]
        last = vout_ref[60:61, :] * scale
        o_wl[0:1, :] = last[:, 0:64]
        o_wl[1:2, :] = last[:, 64:128]
        o_bl[...] = jnp.sum(vout_ref[61:63, :], axis=1, keepdims=True) * scale
        o_b1[...] = vout_ref[63:65, :] * scale
        b2 = vout_ref[65:66, :] * scale
        o_b2[0:1, :] = b2[:, 0:64]
        o_b2[1:2, :] = b2[:, 64:128]


def on_device(
    features, validity, labels, expert_in, expert_in_bias, norm_gain, norm_bias, expert_out,
    expert_out_bias, gate_weight, gate_bias, tower_first, tower_first_bias, tower_second,
    tower_second_bias, tower_last, tower_last_bias,
):
    rows = features.shape[0]
    R = rows // 2
    n_batch = lax.axis_size("batch")
    plan = plan_of(n_batch)
    n_levels = len(plan)
    n_peers = sum(radix - 1 for _, radix, _, _ in plan)
    n_sems = 1 + 2 * n_peers
    v_row = validity.reshape(1, rows)
    y_rows = labels.T
    vm = pl.BlockSpec(memory_space=pltpu.VMEM)
    sm = pl.BlockSpec(memory_space=pltpu.SMEM)
    hb = pl.BlockSpec(memory_space=pl.ANY)
    dma = pltpu.SemaphoreType.DMA

    def scr(*shape, dtype=F32):
        return pltpu.VMEM(shape, dtype)

    scratch = [
        scr(R, D, dtype=BF16), scr(E * H, R, dtype=BF16), scr(E * H, R, dtype=BF16),
        scr(E * H, R, dtype=BF16), scr(8, R), scr(16, R, dtype=BF16), scr(2, R),
        scr(E * H + 32, D, dtype=BF16), scr(D, E * H, dtype=BF16), scr(D, 128, dtype=BF16),
        scr(E * H, H, dtype=BF16), scr(E * H, H, dtype=BF16),
        scr(E * H, 128), scr(E * H, 128), scr(E * H, 128), scr(E * H, 128), scr(E * H, 128),
        scr(2, 128, H, dtype=BF16), scr(2, H, 128, dtype=BF16), scr(128, H, dtype=BF16),
        scr(H, 128, dtype=BF16), scr(H, 128), scr(128, 128), scr(128, 128), scr(8, 128),
        scr(E * H, TF), scr(E * H, TF), scr(2 * H, TF, dtype=BF16), scr(H, TF, dtype=BF16), scr(2 * H, TF),
        scr(H, D), scr(H, H), scr(16, D), scr(2, H, 128), scr(128, H),
        scr(3, H, 128), scr(8, 128), scr(8, 128), scr(128, 128), scr(128, 128), scr(H, 128),
        scr(1, D), scr(4, 8, H),
        scr(24, 128), scr(24, 128),
        scr(2, 8, D), scr(n_levels, 4, 8, D), scr(2, VR, 128), scr(n_levels, 4, VR, 128),
        scr(2, H, CW), scr(NC, H, CW, dtype=BF16),
        [scr(NC, radix, after, CW, dtype=BF16) for _, radix, _, after in plan],
        dma((8,)), dma((8,)), dma((2 + 6 * n_levels,)), dma((2 + 6 * n_levels,)),
        dma((NC, n_sems)), dma((NC, n_sems)), dma((12,)), dma((8,)),
    ]
    flops = 2 * R * (6 * D * E * H // 2 + 3 * E * H * H)
    d_half, preds, gsum, vsum, stats = pl.pallas_call(
        functools.partial(main_kernel, plan, R),
        out_shape=(
            jax.ShapeDtypeStruct((256, rows), BF16),
            jax.ShapeDtypeStruct((2, rows), F32),
            jax.ShapeDtypeStruct((NC, H, CW), BF16),
            jax.ShapeDtypeStruct((VR, 128), F32),
            jax.ShapeDtypeStruct((8, D), F32),
        ),
        in_specs=[hb] + [vm] * 9 + [sm] + [vm] * 5 + [sm],
        out_specs=(hb, hb, hb, vm, vm),
        scratch_shapes=scratch,
        compiler_params=pltpu.CompilerParams(
            collective_id=0, has_side_effects=True, vmem_limit_bytes=64 * 2**20 - 65536
        ),
        cost_estimate=pl.CostEstimate(flops=flops, bytes_accessed=20 * 2**20, transcendentals=0),
        name="layer",
    )(
        features, v_row, y_rows, expert_in, expert_out, expert_in_bias, norm_gain, norm_bias,
        expert_out_bias, jnp.swapaxes(gate_weight, 1, 2), gate_bias, tower_first, tower_first_bias,
        jnp.swapaxes(tower_second, 1, 2), tower_second_bias, tower_last, tower_last_bias,
    )

    tile = 512
    whole = lambda *shape: pl.BlockSpec(shape, lambda i: (0,) * len(shape))
    half_index = lambda i: (i, lax.axis_index("mp"))
    out_shapes = [
        (2, rows), (rows, 256), (E, D, 128), (E, 128), (E, 128), (E, 128), (E, 128, H), (E, H),
        (2, 4, D), (2, 4), (2, H, 128), (2, 128), (2, 64, 128), (2, 64), (2, 64), (2, 128),
    ]
    out_specs = [whole(*shape) for shape in out_shapes]
    out_specs[1] = pl.BlockSpec((tile, 256), lambda i: (i, 0))
    outs = pl.pallas_call(
        functools.partial(final_kernel, tile),
        grid=(rows // tile,),
        out_shape=[jax.ShapeDtypeStruct(shape, F32) for shape in out_shapes],
        in_specs=[
            pl.BlockSpec((256, tile), lambda i: (0, i)),
            pl.BlockSpec((tile, 256), half_index),
            pl.BlockSpec((1, tile), lambda i: (0, i)),
            whole(2, rows), whole(NC, H, CW), whole(VR, 128), whole(8, D),
        ],
        out_specs=out_specs,
        compiler_params=pltpu.CompilerParams(vmem_limit_bytes=48 * 2**20),
        cost_estimate=pl.CostEstimate(
            flops=rows * 256 * 8, bytes_accessed=rows * 256 * 8, transcendentals=0
        ),
        name="finish",
    )(d_half, features, v_row, preds, gsum, vsum, stats)
    outs = list(outs)
    outs[0] = outs[0].T
    outs[8] = jnp.swapaxes(outs[8], 1, 2)
    outs[12] = jnp.swapaxes(outs[12], 1, 2)
    outs[15] = outs[15][:, 0]
    return tuple(outs)


def solution(mesh):
    in_specs = (
        P("batch", None), P("batch"), P("batch", None), P(None, None, "mp"), P(None, "mp"),
        P(None, "mp"), P(None, "mp"), P(None, "mp", None), P(), P(), P(), P(), P(), P(), P(), P(), P(),
    )
    out_specs = (
        P("batch", None), P("batch", "mp"), P(None, None, "mp"), P(None, "mp"), P(None, "mp"),
        P(None, "mp"), P(None, "mp", None), P(), P(), P(), P(), P(), P(), P(), P(), P(),
    )
    return jax.shard_map(
        on_device, mesh=mesh, in_specs=in_specs, out_specs=out_specs, check_vma=False
    )
```

time: 916 us -> 164 us (0.18); the launches traced: 906 us -> 164 us
  matrix products: 312 us -> 0 us
  other arithmetic: 209 us -> 0 us
  waiting for transfers between devices: 199 us -> 0 us
  blocking collectives: 158 us -> 0 us
  Pallas kernels: 0 us -> 156 us
  between operations: 15.2 us -> 0.68 us
    dot_general x25 -> x0, matrix products: 291 us -> none  [the longest x2 48.3 us: on_device(): grad_first.append(jnp.dot(mixed.T, d_first, precision=HIGHEST))]
    psum x3 -> x0, blocking collectives: 158 us -> none  [the longest x1 77.2 us: on_device(): lax.psum((jnp.sum(normed_gradient_local, axis=0), jnp.sum(normed_gradient...]
    pallas_call x0 -> x2, Pallas kernels: none -> 156 us  [the longest x1 142 us: on_device(): pl.pallas_call(functools.partial(main_kernel, plan, R), out_shape=(jax.Sh...]
    psum x3 -> x0, waiting for transfers between devices: 92.3 us -> none  [the longest x1 63 us: on_device(): summed_all = lax.psum(expert_terms + head_terms, 'batch')]
    reduce_sum x11 -> x0, other arithmetic: 76.2 us -> none  [the longest x1 19.9 us: on_device(): grad_in_b = jnp.sum(d_pre_low.astype(jnp.float32), axis=1)]
    reduce_scatter x2 -> x0, waiting for transfers between devices: 72.9 us -> none  [the longest x1 64.6 us: on_device(): lax.psum_scatter(partial_out, 'mp', scatter_dimension=2, tiled=True)]
    convert_element_type x7 -> x0, other arithmetic: 58.6 us -> none  [the longest x1 27.1 us: on_device(): outputs_f = outputs.astype(jnp.float32)]
    all_gather x1 -> x0, waiting for transfers between devices: 33.2 us -> none  [on_device(): outputs = lax.all_gather(own_low, 'mp', axis=2, tiled=True)]
  transfers between devices with their start and end apart: 6 -> 0, of which waited for: 6 -> 0; matrix products, arithmetic and copies ran while one was open for 11% -> 0% of each run, Pallas kernels for 0% -> 0%
where the time goes in v1:
time: 164 us
  Pallas kernels  156 us (95%)
  local copies, waits for them, and re-layouts  7.23 us (4%)
    pallas_call x1, Pallas kernels, on_device(): pl.pallas_call(functools.partial(main_kernel, plan, R), out_shape=(jax.Sh...  142 us
    pallas_call x1, Pallas kernels, on_device(): pl.pallas_call(functools.partial(final_kernel, tile), grid=(rows // tile,...  13.8 us
    unnamed x12, local copies, waits for them, and re-layouts  6.6 us

profile of v1, /device:TPU:0, one launch (start us, length us, event | category | flops | bytes accessed | tf_op | source)
XLA Modules:
  0.0 163.7 jit_solution(16151711232653297998)
XLA Ops:
  0.7 142.0 %layer.1 = (bf16[256,8192]{1,0:T(8,128)(2,1)}, f32[2,8192]{1,0:T(2,128)}, bf16[7,256,384]{2,1,0:T(8,128)(2,1)}, f32[72,128]{1,0:T(8,128)}, f32[8,512]{1,0:T(8,128)}) custom-call(bf16[8192,512]{1,0:T(8,128)(2,1)} %x_ref.1, s32[1,8192]{1,0:T(1,128)} %bitcast.7, s32[2,8192]{1,0:T(2,128)} %bitcast.9, f32[6,512,128]{2,1,0:T(8,128)} %win_ref.1, ...), custom_call_target="tpu_custom_call" | custom-call | flops 28991029248 | bytes 20971520 | tf_op jit(solution)/shard_map/layer/pallas_call | solution.py:818
  142.7 0.0 copy-start
  142.7 2.2 %copy-done = bf16[256,8192]{1,0:T(8,128)(2,1)S(1)} copy-done((bf16[256,8192]{1,0:T(8,128)(2,1)S(1)}, bf16[256,8192]{1,0:T(8,128)(2,1)}, u32[]{:S(2)}) %copy-start) | copy-done | bytes 4194328
  144.9 0.0 copy-start.1
  144.9 1.3 copy-done.1
  146.2 0.0 copy-start.2
  146.2 0.8 copy-done.2
  147.0 0.0 copy-start.3
  147.0 0.8 copy-done.3
  147.8 0.0 copy-start.4
  147.8 0.8 copy-done.4
  148.6 0.0 copy-start.5
  148.6 0.7 copy-done.5
  149.3 13.8 %finish.1 = (f32[2,8192]{1,0:T(2,128)}, f32[8192,256]{1,0:T(8,128)}, f32[6,512,128]{2,1,0:T(8,128)}, f32[6,128]{1,0:T(8,128)}, f32[6,128]{1,0:T(8,128)}, /*index...) custom-call(bf16[256,8192]{1,0:T(8,128)(2,1)S(1)} %copy-done, ...), custom_call_target="tpu_custom_call" | custom-call | flops 16777216 | bytes 16777216 | tf_op jit(solution)/shard_map/finish/pallas_call | solution.py:850
  163.1 0.6 slice_reduce_fusion
Async XLA Ops:
  142.7 2.2 %copy-start = (bf16[256,8192]{1,0:T(8,128)(2,1)S(1)}, bf16[256,8192]{1,0:T(8,128)(2,1)}, u32[]{:S(2)}) copy-start(bf16[256,8192]{1,0:T(8,128)(2,1)} %get-tuple-element.37.dt_ref) | copy-start | bytes 12582916
  144.9 1.3 copy-start.1
  146.2 0.8 copy-start.2
  147.0 0.8 copy-start.3
  147.8 0.8 copy-start.4
  148.6 0.7 copy-start.5

commit v2 on v1

--- a/solution.py
+++ b/solution.py
@@ -20,8 +20,10 @@
 SB = 256
 CH = 32
 VR = 72
-CW = 384
-NC = E + 1
+HE = H + 16
+WIDTHS = (256,) * E + (384,) * 3
+NC = len(WIDTHS)
+TOWERS = E
 
 
 def levels_of(count):
@@ -97,20 +99,26 @@
 
 def main_kernel(
     plan, rows_core,
-    x_hbm, v_ref, y_ref, win_ref, wout_ref, bin_ref, gain_ref, nb_ref, bout_ref, gate_ref, gb_ref,
+    x_hbm, v_ref, y_ref, win_hbm, wout_hbm, bin_ref, gain_ref, nb_ref, bout_ref, gate_ref, gb_ref,
     w1_ref, b1_ref, w2_ref, b2_ref, wl_ref, bl_ref,
-    d_hbm, pred_hbm, gout_hbm, vout_ref, stat_ref,
-    xbuf, zbuf, hbuf, dobuf, rbuf, dlogbuf, predbuf,
-    wf, wb, gback, wot, wo, bct, g2t, b2t, gt, bot,
+    d_hbm, pred_hbm, gout_hbm, vout_ref, stat_ref, wb_hbm,
+    xbuf, zbuf, sbuf, dobuf, rbuf, dlogbuf, predbuf,
+    wf, gback, wot, pk, g2t, b2t,
     w1t, w1n, w2f, w2b, b1t, b2tt, wlt, gbt,
-    abuf, obuf, mixb, u1b, dmix,
-    acc_in, acc_out, acc_gate, acc_first, acc_second,
-    acc_u, acc_dlog, acc_lb, acc_last, acc_b2, acc_b1, s2row, vec,
+    abufs, hbufs, logit_bufs, mixb, u1b, dmix,
+    acc_out, acc_gate, acc_first, acc_second,
+    acc_dlog, acc_lb, acc_last, acc_b2, acc_b1, s2row,
     bias_snd, bias_rcv,
-    st_mp, st_lv, v_mp, v_lv, hkeep, mprecv, lvrecv,
-    sem_x, sem_w, sem_st, sem_v, sem_s, sem_r, sem_l, sem_d,
+    st_mp, st_lv, v_mp, v_lv, sends, sends_low, mprecv, lvrecv,
+    sem_x, sem_w, sem_st, sem_v, sem_s, sem_r, sem_l, sem_d, sem_f,
 ):
     R = rows_core
+    abuf = abufs[0]
+    acc_in = (abuf.at[0:H, :], abuf.at[H : 2 * H, :])
+    hkeep = (abuf.at[2 * H : 3 * H, :], abuf.at[3 * H : 4 * H, :])
+    acc_u = (
+        abuf.at[4 * H : 5 * H, 0:128], abuf.at[4 * H : 5 * H, 128:256], abuf.at[5 * H : 6 * H, 0:128]
+    )
     n_levels = len(plan)
     b = lax.axis_index("batch")
     mp = lax.axis_index("mp")
@@ -142,6 +150,24 @@
         copy.start()
         x_copies.append(copy)
 
+    f_copies = []
+    for e in range(E):
+        for k in range(2):
+            f_copies.append(
+                pltpu.make_async_copy(
+                    win_hbm.at[e, k * H : (k + 1) * H, :],
+                    abuf.at[e * H : (e + 1) * H, k * 128 : (k + 1) * 128],
+                    sem_f.at[2 * e + k],
+                )
+            )
+        f_copies.append(
+            pltpu.make_async_copy(
+                wout_hbm.at[e], acc_out.at[e * 128 : (e + 1) * 128, :], sem_f.at[2 * E + e]
+            )
+        )
+    for copy in f_copies:
+        copy.start()
+
     barrier = pltpu.get_barrier_semaphore()
     greets = [(b, other)]
     for level in range(n_levels):
@@ -154,9 +180,14 @@
     win_rcv = dobuf.at[0:D, 1024 : 1024 + E * 128]
     wout_snd = dobuf.at[D : D + 128, 0 : E * H]
     wout_rcv = dobuf.at[D : D + 128, 2048 : 2048 + E * H]
+    for copy in f_copies:
+        copy.wait()
     for e in range(E):
-        win_snd[:, e * 128 : (e + 1) * 128] = win_ref[e].astype(BF16)
-        wout_snd[:, e * H : (e + 1) * H] = wout_ref[e].astype(BF16)
+        for k in range(2):
+            win_snd[k * H : (k + 1) * H, e * 128 : (e + 1) * 128] = abuf[
+                e * H : (e + 1) * H, k * 128 : (k + 1) * 128
+            ].astype(BF16)
+        wout_snd[:, e * H : (e + 1) * H] = acc_out[e * 128 : (e + 1) * 128, :].astype(BF16)
     bias_snd[0:E] = bin_ref[...]
     bias_snd[8 : 8 + E] = gain_ref[...]
     bias_snd[16 : 16 + E] = nb_ref[...]
@@ -190,20 +221,15 @@
 
     for t in range(2):
         w1n[t] = w1_ref[t].astype(BF16)
-        w1t[t] = w1_ref[t].T.astype(BF16)
-        b1t[t * 128 : (t + 1) * 128] = column(b1_ref[t : t + 1, :])
-        for k in range(2):
-            for e in range(3 * t, 3 * t + 3):
-                bot[e * H + k * 128 : e * H + (k + 1) * 128] = column(
-                    bout_ref[e : e + 1, k * 128 : (k + 1) * 128]
-                )
+        w1t[t] = (w1_ref[t].T * 0.5).astype(BF16)
+        b1t[t * 128 : (t + 1) * 128] = column(b1_ref[t : t + 1, :]) * 0.5
     zero64 = jnp.zeros((64, 128), F32)
     zero128 = jnp.zeros((128, 64), F32)
-    w2f[0:64] = jnp.concatenate([w2_ref[0], zero64], axis=1).astype(BF16)
-    w2f[64:128] = jnp.concatenate([zero64, w2_ref[1]], axis=1).astype(BF16)
-    w2b[0:128] = jnp.concatenate([w2_ref[0].T, zero128], axis=1).astype(BF16)
-    w2b[128:256] = jnp.concatenate([zero128, w2_ref[1].T], axis=1).astype(BF16)
-    b2tt[...] = column(jnp.concatenate([b2_ref[0:1, :], b2_ref[1:2, :]], axis=1))
+    w2f[0:64] = (jnp.concatenate([w2_ref[0], zero64], axis=1) * 0.5).astype(BF16)
+    w2f[64:128] = (jnp.concatenate([zero64, w2_ref[1]], axis=1) * 0.5).astype(BF16)
+    w2b[0:128] = (jnp.concatenate([w2_ref[0].T, zero128], axis=1) * 0.5).astype(BF16)
+    w2b[128:256] = (jnp.concatenate([zero128, w2_ref[1].T], axis=1) * 0.5).astype(BF16)
+    b2tt[...] = column(jnp.concatenate([b2_ref[0:1, :], b2_ref[1:2, :]], axis=1)) * 0.5
     wlt[...] = column(jnp.concatenate([wl_ref[0:1, :], wl_ref[1:2, :]], axis=1))
     gbt[...] = jnp.concatenate(
         [jnp.full((1, 128), gb_ref[t, k], F32) for t in range(2) for k in range(4)], axis=0
@@ -212,6 +238,10 @@
     gate_low = gate.astype(BF16).astype(F32)
     gback[...] = jnp.concatenate([gate_low, gate_low, jnp.zeros((112, D), F32)], axis=0).T.astype(BF16)
     acc_gate[...] = jnp.zeros_like(acc_gate)
+    acc_out[...] = jnp.zeros_like(acc_out)
+    for hbuf in hbufs:
+        for e in range(E):
+            hbuf[e * HE + H : (e + 1) * HE, :] = jnp.ones((16, TF), BF16)
     acc_first[...] = jnp.zeros_like(acc_first)
     acc_second[...] = jnp.zeros_like(acc_second)
     acc_dlog[...] = jnp.zeros_like(acc_dlog)
@@ -220,18 +250,17 @@
     acc_b1[...] = jnp.zeros_like(acc_b1)
     acc_b2[...] = jnp.zeros_like(acc_b2)
 
+    lane = lax.broadcasted_iota(jnp.int32, (128, 128), 1)
+
     def place(half, win, wout, bias):
         for e in range(E):
             at = pl.multiple_of(e * H + half * 128, 128)
             w = win[:, e * 128 : (e + 1) * 128]
-            wb[:, pl.ds(at, 128)] = w
             wf[pl.ds(at, 128), :] = w.T
             o = wout[:, e * H : (e + 1) * H]
-            wo[pl.ds(at, 128), :] = (o.astype(F32) * 0.5).astype(BF16)
             wot[pl.ds(e * H, H), pl.ds(pl.multiple_of(half * 128, 128), 128)] = o.T
-            bct[pl.ds(at, 128), :] = column(bias[e : e + 1, :])
             gain = column(bias[8 + e : 9 + e, :])
-            gt[pl.ds(at, 128), :] = gain
+            pk[pl.ds(at, 128), :] = jnp.where(lane == 0, column(bias[e : e + 1, :]), gain)
             g2t[pl.ds(at, 128), :] = gain * 0.5
             b2t[pl.ds(at, 128), :] = column(bias[16 + e : 17 + e, :]) * 0.5
 
@@ -255,12 +284,23 @@
             for copy in w_copies:
                 copy.wait()
             place(other, win_rcv, wout_rcv, bias_rcv)
+            keep = [
+                pltpu.make_async_copy(win_snd, wb_hbm.at[mp], sem_f.at[0]),
+                pltpu.make_async_copy(win_rcv, wb_hbm.at[other], sem_f.at[1]),
+            ]
+            for copy in keep:
+                copy.start()
             means = []
             for e in range(E):
                 w = wf[e * H : (e + 1) * H, :].astype(F32)
                 means.append(jnp.sum(w, axis=0, keepdims=True) * (1.0 / H))
-                shift = jnp.sum(bct[e * H : (e + 1) * H, :], axis=0, keepdims=True) * (1.0 / H)
-                bct[e * H : (e + 1) * H, :] = bct[e * H : (e + 1) * H, :] - shift
+                shift = jnp.sum(pk[e * H : (e + 1) * H, 0:1], axis=0, keepdims=True) * (1.0 / H)
+                for k in range(2):
+                    at = slice(e * H + k * 128, e * H + (k + 1) * 128)
+                    table = pk[at, :]
+                    table = jnp.where(lane == 0, table - shift, table)
+                    second = column(bout_ref[e : e + 1, k * 128 : (k + 1) * 128])
+                    pk[at, :] = jnp.where(lane == 1, second, table)
             pad = [jnp.zeros((2, D), F32)]
             means = jnp.concatenate(means + pad, axis=0)
             means_high = means.astype(BF16).astype(F32)
@@ -274,36 +314,57 @@
     inv = lax.rsqrt(square / count + EPS)
     stat_ref[...] = jnp.concatenate([mu, inv, count, jnp.zeros((5, D), F32)], axis=0)
 
-    def forward(i):
+    def forward(i, side):
+        abuf, hbuf = abufs[side], hbufs[side]
         r0 = pl.multiple_of(i * TF, TF)
         x_tile = xbuf[pl.ds(r0, TF), :].astype(F32)
         xn = ((x_tile - stat_ref[0:1, :]) * stat_ref[1:2, :]).astype(BF16)
         xbuf[pl.ds(r0, TF), :] = xn
         ext = nt(wf[E * H : E * H + 32, :], xn)
-        for e in range(E):
+        logit_bufs[side][...] = ext[0:8] + wide(gbt[...], TF)
+        means = ext[8:16] + ext[16:24]
+
+        def product(e):
             abuf[e * H : (e + 1) * H, :] = nt(wf[e * H : (e + 1) * H, :], xn)
-        for e in range(E):
-            mean = ext[8 + e : 9 + e] + ext[16 + e : 17 + e]
+
+        def norm(e):
             squares = jnp.zeros((8, TF), F32)
             for at in range(e * H, (e + 1) * H, CH):
-                c = (abuf[at : at + CH, :] - mean) + wide(bct[at : at + CH, :], TF)
+                c = (abuf[at : at + CH, :] - means[e : e + 1]) + pk[at : at + CH, 0:1]
                 abuf[at : at + CH, :] = c
                 squares = squares + fold8(c * c)
             r = lax.rsqrt(jnp.sum(squares, axis=0, keepdims=True) * (1.0 / H) + EPS)
             rbuf[e : e + 1, pl.ds(r0, TF)] = r
-            for at in range(e * H, (e + 1) * H, CH):
+            for u in range(0, H, CH):
+                at = e * H + u
                 zhat = abuf[at : at + CH, :] * r
                 zbuf[at : at + CH, pl.ds(r0, TF)] = zhat.astype(BF16)
                 half = zhat * wide(g2t[at : at + CH, :], TF) + wide(b2t[at : at + CH, :], TF)
-                hbuf[at : at + CH, pl.ds(r0, TF)] = (half * (1.0 + jnp.tanh(half))).astype(BF16)
-            o = nn(wot[e * H : (e + 1) * H, :], hbuf[e * H : (e + 1) * H, pl.ds(r0, TF)])
-            obuf[e * H : (e + 1) * H, :] = o + wide(bot[e * H : (e + 1) * H, :], TF)
-        return ext
-
-    def heads(i, ext):
+                p = 1.0 + jnp.tanh(half)
+                h = half * p
+                hbuf[e * HE + u : e * HE + u + CH, :] = h.astype(BF16)
+                slope = (p + h * (2.0 - p)) * pk[at : at + CH, 2:3]
+                sbuf[at : at + CH, pl.ds(r0, TF)] = slope.astype(BF16)
+
+        def output(e):
+            o = nn(wot[e * H : (e + 1) * H, :], hbuf[e * HE : e * HE + H, :])
+            abuf[e * H : (e + 1) * H, :] = o + pk[e * H : (e + 1) * H, 1:2]
+
+        product(0)
+        product(1)
+        yield
+        for e in range(E):
+            norm(e)
+            if e + 2 < E:
+                product(e + 2)
+            output(e)
+            yield
+
+    def heads(i, side):
+        abuf, hbuf = abufs[side], hbufs[side]
         r0 = pl.multiple_of(i * TF, TF)
         v0 = pl.multiple_of(mp * R + i * TF, 128)
-        logits = ext[0:8] + wide(gbt[...], TF)
+        logits = logit_bufs[side][...]
         probs = []
         for t in range(2):
             part = logits[4 * t : 4 * t + 4]
@@ -315,20 +376,24 @@
                 mixed = None
                 for k in range(4):
                     e = TASK_EXPERTS[t][k]
-                    term = probs[t][k] * obuf[e * H + at : e * H + at + CH, :]
+                    term = probs[t][k] * abuf[e * H + at : e * H + at + CH, :]
                     mixed = term if mixed is None else mixed + term
                 mixb[t * H + at : t * H + at + CH, :] = mixed.astype(BF16)
+        pres = [nn(w1t[t], mixb[t * H : (t + 1) * H, :]) for t in range(2)]
+        yield
         slopes = []
         for t in range(2):
-            pre = nn(w1t[t], mixb[t * H : (t + 1) * H, :])
-            half = (pre + wide(b1t[t * 128 : (t + 1) * 128, :], TF)) * 0.5
+            half = pres[t] + wide(b1t[t * 128 : (t + 1) * 128, :], TF)
             p = 1.0 + jnp.tanh(half)
-            u1b[t * 128 : (t + 1) * 128, :] = (half * p).astype(BF16)
-            slopes.append(0.5 * p * (1.0 + half * (2.0 - p)))
-        half = (nn(w2f[...], u1b[...]) + wide(b2tt[...], TF)) * 0.5
+            u1 = half * p
+            u1b[t * 128 : (t + 1) * 128, :] = u1.astype(BF16)
+            slopes.append(p + u1 * (2.0 - p))
+        pre = nn(w2f[...], u1b[...])
+        yield
+        half = pre + wide(b2tt[...], TF)
         p = 1.0 + jnp.tanh(half)
         u2 = half * p
-        slope2 = 0.5 * p * (1.0 + half * (2.0 - p))
+        slope2 = p + u2 * (2.0 - p)
         wl = wide(wlt[...], TF)
         weighted = u2 * wl
         d_logits = []
@@ -344,17 +409,19 @@
         )
         acc_last[...] += fold_lanes(u2 * d_logit)
         acc_lb[0:2] += fold_lanes(jnp.concatenate(d_logits, axis=0))
-        d2 = d_logit * wl * slope2
+        d2 = (d_logit * 0.5) * (wl * slope2)
         acc_b2[...] += fold_lanes(d2)
         d2_low = d2.astype(BF16)
+        d_u1 = nn(w2b[...], d2_low)
         acc_second[...] += nt(d2_low, u1b[...])
-        d_u1 = nn(w2b[...], d2_low)
+        yield
         for t in range(2):
             d1 = d_u1[t * 128 : (t + 1) * 128] * slopes[t]
             acc_b1[t * 128 : (t + 1) * 128] += fold_lanes(d1)
             d1_low = d1.astype(BF16)
+            dmix[t * H : (t + 1) * H, :] = nn(w1n[t], d1_low)
             acc_first[t] += nt(mixb[t * H : (t + 1) * H, :], d1_low)
-            dmix[t * H : (t + 1) * H, :] = nn(w1n[t], d1_low)
+        yield
         dots = [[jnp.zeros((8, TF), F32) for _ in range(4)] for _ in range(2)]
         for at in range(0, H, CH):
             dm = [dmix[t * H + at : t * H + at + CH, :] for t in range(2)]
@@ -364,7 +431,7 @@
                     e = TASK_EXPERTS[t][k]
                     term = probs[t][k] * dm[t]
                     grads[e] = term if grads[e] is None else grads[e] + term
-                    o = obuf[e * H + at : e * H + at + CH, :]
+                    o = abuf[e * H + at : e * H + at + CH, :]
                     dots[t][k] = dots[t][k] + fold8(dm[t] * o)
             for e in range(E):
                 dobuf[e * H + at : e * H + at + CH, pl.ds(r0, TF)] = grads[e].astype(BF16)
@@ -379,12 +446,32 @@
         d_gate = jnp.concatenate([high, d_gate - high], axis=0).astype(BF16)
         dlogbuf[:, pl.ds(r0, TF)] = d_gate
         acc_gate[...] += nn(d_gate, xbuf[pl.ds(r0, TF), :])
-
-    def forward_step(i, carry):
-        heads(i, forward(i))
+        yield
+        for e in range(E):
+            at = pl.ds(e * HE, HE)
+            acc_out[at, :] += nt(hbuf[at, :], dobuf[e * H : (e + 1) * H, pl.ds(r0, TF)])
+        yield
+
+    def together(*parts):
+        parts = list(parts)
+        while parts:
+            for part in list(parts):
+                if next(part, "end") == "end":
+                    parts.remove(part)
+
+    for copy in keep:
+        copy.wait()
+    n_f = R // TF
+    together(forward(0, 0))
+
+    def forward_pair(j, carry):
+        together(forward(2 * j + 1, 1), heads(2 * j, 0))
+        together(forward(2 * j + 2, 0), heads(2 * j + 1, 1))
         return carry
 
-    lax.fori_loop(0, R // TF, forward_step, 0)
+    lax.fori_loop(0, n_f // 2 - 1, forward_pair, 0)
+    together(forward(n_f - 1, 1), heads(n_f - 2, 0))
+    together(heads(n_f - 1, 1))
 
     pending = []
     pred_at = pl.ds(pl.multiple_of(mp * R, 128), R)
@@ -397,20 +484,24 @@
     n_sems = 1 + 2 * sum(radix - 1 for _, radix, _, _ in plan)
 
     def source(c, rows, place_at):
-        base = 2048 if c == E else 0
-        e = 0 if c == E else c
-        return hbuf.at[pl.ds(e * H, rows), pl.ds(base + place_at * CW, CW)]
+        w = WIDTHS[c]
+        at = sum(p[2] for p in plan[1:place_at])
+        if c < E:
+            return sbuf.at[pl.ds(c * H + at, rows), pl.ds(min(place_at, 1) * w, w)]
+        if place_at:
+            return sends_low.at[c - E, pl.ds(at, rows), :]
+        return sends.at[c - E, pl.ds(0, rows), :]
 
     def level_sems(level):
         return 1 + 2 * sum(radix - 1 for _, radix, _, _ in plan[:level])
 
     def start_pair(c):
         src = source(c, H, 0)
-        flight[c] = [send(src, mprecv.at[c], sem_s.at[c, 0], sem_r.at[c, 0], (b, other))]
+        flight[c] = [send(src, mprecv[c], sem_s.at[c, 0], sem_r.at[c, 0], (b, other))]
 
     def start_level(c, level, value):
         stride, radix, rows, after = plan[level]
-        out = source(c, rows, 1 + level)
+        out = source(c, rows, level)
         out[...] = value.astype(BF16)
         copies = []
         for step in range(1, radix):
@@ -419,26 +510,26 @@
             if after != rows:
                 to = lax.rem(digits[level] + step, radix)
                 part = out.at[pl.ds(pl.multiple_of(to * after, 16), after), :]
-            dst = lvrecv[level].at[c, step]
+            dst = lvrecv[c][level].at[step]
             copies.append(send(part, dst, sem_s.at[c, k], sem_r.at[c, k], peer(level, step)))
         flight[c] = copies
         if after != rows:
             mine = out[pl.ds(pl.multiple_of(digits[level] * after, 16), after), :]
         else:
             mine = out[...]
-        lvrecv[level][c, 0] = mine
+        lvrecv[c][level][0] = mine
 
     def finish_level(c, level):
         stride, radix, rows, after = plan[level]
         for copy in flight[c]:
             copy.wait()
         if after != rows:
-            parts = [lvrecv[level][c, step].astype(F32) for step in range(radix)]
+            parts = [lvrecv[c][level][step].astype(F32) for step in range(radix)]
             return functools.reduce(lambda p, q: p + q, parts)
         total = None
         for k in range(radix):
             step = lax.rem(k - digits[level] + radix, radix)
-            part = lvrecv[level][c, step].astype(F32)
+            part = lvrecv[c][level][step].astype(F32)
             total = part if total is None else total + part
         return total
 
@@ -449,14 +540,14 @@
                 at = at + digits[k] * plan[k][3]
         rows = plan[level][3] if level >= 0 else H
         if isinstance(at, int):
-            return gout_hbm.at[c, pl.ds(at, rows), :]
-        return gout_hbm.at[c, pl.ds(pl.multiple_of(at, 16), rows), :]
+            return gout_hbm.at[c, pl.ds(at, rows), pl.ds(0, WIDTHS[c])]
+        return gout_hbm.at[c, pl.ds(pl.multiple_of(at, 16), rows), pl.ds(0, WIDTHS[c])]
 
     split = [level for level in range(n_levels) if plan[level][2] != plan[level][3]]
 
     def start_result(c, value):
         rows = plan[-1][3]
-        final = source(c, rows, 1 + n_levels)
+        final = source(c, rows, n_levels)
         final[...] = value.astype(BF16)
         local = pltpu.make_async_copy(final, region(c, n_levels - 1), sem_l.at[1 + c])
         local.start()
@@ -477,10 +568,12 @@
             for copy in flight[c]:
                 copy.wait()
             if c < E:
-                value = hkeep[c % 2] + mprecv[c].astype(F32)
+                value = hkeep[c % 2][...]
+            elif c == TOWERS:
+                value = source(c, H, 0)[...].astype(F32)
             else:
-                value = source(c, H, 0)[...].astype(F32) + mprecv[c].astype(F32)
-            start_level(c, 0, value)
+                value = half_out(c - TOWERS - 1, mp)
+            start_level(c, 0, value + mprecv[c][...].astype(F32))
 
         steps.append(from_pair)
         for level in range(n_levels):
@@ -512,15 +605,33 @@
         return steps
 
     queue = []
+    clock = [0]
+
+    def start_steps(steps, spacing):
+        queue.append([clock[0] + spacing, spacing, steps])
 
     def turn():
-        for steps in list(queue):
-            steps.pop(0)()
-            if not steps:
-                queue.remove(steps)
+        clock[0] += 1
+        for item in list(queue):
+            if clock[0] >= item[0]:
+                item[2].pop(0)()
+                item[0] = clock[0] + item[1]
+                if not item[2]:
+                    queue.remove(item)
+
+    def half_out(group, h):
+        parts = []
+        for e in range(3 * group, 3 * group + 3):
+            a = acc_out[pl.ds(pl.multiple_of(e * HE + h * 128, 16), 128), :]
+            parts.append(jnp.concatenate([a[:, 0:128], a[:, 128:256]], axis=0))
+        return jnp.concatenate(parts, axis=1)
+
+    def half_in(h):
+        at = pl.ds(pl.multiple_of(h * 128, 128), 128)
+        return jnp.concatenate([acc_in[0][at, :], acc_in[1][at, :]], axis=0)
 
     def pack_towers():
-        src = source(E, H, 0)
+        src = source(TOWERS, H, 0)
         src[:, 0:128] = acc_first[0].astype(BF16)
         src[:, 128:256] = acc_first[1].astype(BF16)
         gates = acc_gate[0:8] + acc_gate[8:16]
@@ -529,96 +640,143 @@
         rest.append(jnp.zeros((H - 160, 128), F32))
         src[:, 256:384] = jnp.concatenate(rest, axis=0).astype(BF16)
 
-    def pack_expert(e):
-        def half(h):
-            at = pl.ds(pl.multiple_of(h * 128, 128), 128)
-            a, o = acc_in[at, :], acc_out[at, :]
-            top = jnp.concatenate([a[:, 0:256], o[:, 0:128]], axis=1)
-            low = jnp.concatenate([a[:, 256:512], o[:, 128:256]], axis=1)
-            return top, low
-
-        top, low = half(mp)
-        hkeep[e % 2, 0:128] = top
-        hkeep[e % 2, 128:256] = low
-        src = source(e, H, 0)
-        top, low = half(other)
-        src[0:128, :] = top.astype(BF16)
-        src[128:256, :] = low.astype(BF16)
-
-    ones16 = jnp.ones((16, SB), BF16)
+    def launch(c, spacing=3):
+        start_pair(c)
+        start_steps(chunk_steps(c), spacing)
+
+    pack_towers()
+    launch(TOWERS)
+
+    def launch_out(group):
+        source(TOWERS + 1 + group, H, 0)[...] = half_out(group, other).astype(BF16)
+        launch(TOWERS + 1 + group)
+
     s2row[...] = jnp.sum(
         (gate_low * (acc_gate[0:8] + acc_gate[8:16])), axis=0, keepdims=True
     )
 
-    def backward_part(e, r0):
+    def backward_start(e, i):
+        rows = slice(e * H, (e + 1) * H)
+        for part in range(TB // SB):
+            lanes = pl.ds(pl.multiple_of(i * TB + part * SB, SB), SB)
+            dmix[part * H : (part + 1) * H, :] = nn(wot[rows, :], dobuf[rows, lanes])
+
+    def backward_part(e, r0, part):
         at0 = e * H
         lanes = pl.ds(r0, SB)
-        do = dobuf[at0 : at0 + H, lanes]
-        dmix[0:H, :] = nn(wo[at0 : at0 + H, :], do)
-        acc_out[...] += nt(hbuf[at0 : at0 + H, lanes], do)
-        vec[3] += nt(ones16, do)[0:8]
+        work = dmix.at[part * H : (part + 1) * H]
         r = rbuf[e : e + 1, lanes]
         m1 = jnp.zeros((8, SB), F32)
         m2 = jnp.zeros((8, SB), F32)
         for u in range(0, H, CH):
             at = at0 + u
             zhat = zbuf[at : at + CH, lanes].astype(F32)
-            half = zhat * wide(g2t[at : at + CH, :], SB) + wide(b2t[at : at + CH, :], SB)
-            p = 1.0 + jnp.tanh(half)
-            dz = dmix[u : u + CH, :] * (p * (1.0 + half * (2.0 - p)))
-            q = dz * zhat
-            acc_u[0, u : u + CH, :] += fold_lanes(dz)
-            acc_u[1, u : u + CH, :] += fold_lanes(q)
-            g = wide(gt[at : at + CH, :], SB)
-            dzg = dz * g
-            dmix[u : u + CH, :] = dzg
+            dzg = work[u : u + CH, :] * sbuf[at : at + CH, lanes].astype(F32)
+            q = dzg * zhat
+            acc_u[0][u : u + CH, :] += fold_lanes(dzg)
+            acc_u[1][u : u + CH, :] += fold_lanes(q)
+            work[u : u + CH, :] = dzg
             m1 = m1 + fold8(dzg)
-            m2 = m2 + fold8(q * g)
+            m2 = m2 + fold8(q)
         m1 = jnp.sum(m1, axis=0, keepdims=True) * (1.0 / H)
         m2 = jnp.sum(m2, axis=0, keepdims=True) * (1.0 / H)
         for u in range(0, H, CH):
             at = at0 + u
             zhat = zbuf[at : at + CH, lanes].astype(F32)
-            da = r * (dmix[u : u + CH, :] - m1 - zhat * m2)
-            acc_u[2, u : u + CH, :] += fold_lanes(da)
+            da = r * (work[u : u + CH, :] - m1 - zhat * m2)
+            acc_u[2][u : u + CH, :] += fold_lanes(da)
             zbuf[at : at + CH, lanes] = da.astype(BF16)
-        acc_in[...] += nn(zbuf[at0 : at0 + H, lanes], xbuf[pl.ds(r0, SB), :])
-
-    for e in range(E):
-        acc_in[...] = jnp.zeros_like(acc_in)
-        acc_out[...] = jnp.zeros_like(acc_out)
-        acc_u[...] = jnp.zeros_like(acc_u)
-        vec[3] = jnp.zeros((8, H), F32)
-
-        def backward_step(i, carry, e=e):
-            for part in range(TB // SB):
-                backward_part(e, pl.multiple_of(i * TB + part * SB, SB))
-            return carry
-
-        n_b = R // TB
-        lax.fori_loop(0, n_b // 2, backward_step, 0)
-        turn()
-        lax.fori_loop(n_b // 2, n_b, backward_step, 0)
-        turn()
-        if e == 0:
-            pack_towers()
-            start_pair(E)
-            queue.append(chunk_steps(E))
-        pack_expert(e)
-        start_pair(e)
-        queue.append(chunk_steps(e))
-        for k, row in ((0, 2), (1, 1), (2, 0)):
-            sums = lane_sums(acc_u[row])
+
+    n_b = R // TB
+
+    def weight_part(e, i):
+        r0 = pl.multiple_of(i * TB, TB)
+        rows = slice(e * H, (e + 1) * H)
+        grad = nn(zbuf[rows, pl.ds(r0, TB)], xbuf[pl.ds(r0, TB), :])
+        acc_in[0][...] += grad[:, 0:256]
+        acc_in[1][...] += grad[:, 256:512]
+
+    def backward_tile(e, i):
+        for part in range(TB // SB):
+            backward_part(e, pl.multiple_of(i * TB + part * SB, SB), part)
+
+    def clear_units():
+        for part in acc_u:
+            part[...] = jnp.zeros((H, 128), F32)
+
+    def clear_weights():
+        for part in acc_in:
+            part[...] = jnp.zeros((H, 256), F32)
+
+    def finish_units(e):
+        rows = slice(e * H, (e + 1) * H)
+        for k in range(3):
+            part = acc_u[2 - k][...]
+            sums = lane_sums(part / pk[rows, 2:3] if k else part)
             v_mp[mp, k * 12 + 2 * e : k * 12 + 2 * e + 1, :] = sums[:, 0:128]
             v_mp[mp, k * 12 + 2 * e + 1 : k * 12 + 2 * e + 2, :] = sums[:, 128:256]
-        bo = vec[3][0:1]
+        bo = acc_out[e * HE + H : e * HE + H + 1, :]
         v_mp[mp, 36 + 2 * e : 37 + 2 * e, :] = bo[:, 0:128]
         v_mp[mp, 37 + 2 * e : 38 + 2 * e, :] = bo[:, 128:256]
+        clear_units()
+
+    def finish_expert(e):
+        hkeep[e % 2][...] = half_in(mp)
+        source(e, H, 0)[...] = half_in(other).astype(BF16)
+        launch(e, 2 if e >= E - 2 else 3)
         cross = jnp.zeros((8, D), F32)
         for u in range(0, H, CH):
             w = wf[e * H + u : e * H + u + CH, :].astype(F32)
-            cross = cross + fold8(w * acc_in[u : u + CH, :])
+            grad = jnp.concatenate([acc_in[0][u : u + CH, :], acc_in[1][u : u + CH, :]], axis=1)
+            cross = cross + fold8(w * grad)
         s2row[...] += jnp.sum(cross, axis=0, keepdims=True)
+        clear_weights()
+
+    clear_weights()
+    clear_units()
+    for e in range(E):
+        rows = slice(e * H, (e + 1) * H)
+        wot[rows, :] = (wot[rows, :].T.astype(F32) * 0.5).astype(BF16)
+    for e in range(E):
+
+        def backward_step(i, carry, e=e):
+            backward_start(e, i)
+            weight_part(e, i - 1)
+            backward_tile(e, i)
+            return carry
+
+        backward_start(e, 0)
+        if e:
+            weight_part(e - 1, n_b - 1)
+        backward_tile(e, 0)
+        if e:
+            finish_expert(e - 1)
+        if e == 2:
+            back = []
+            for k in range(2 * E):
+                half, to = k % 2, 2048 + k * 128
+                copy = pltpu.make_async_copy(
+                    wb_hbm.at[half, :, (k // 2) * 128 : (k // 2 + 1) * 128],
+                    sbuf.at[0:D, to : to + 128],
+                    sem_f.at[k],
+                )
+                copy.start()
+                back.append(copy)
+        turn()
+        if e == 0:
+            launch_out(0)
+        for k in range(3):
+            first, last = 1 + k * (n_b - 1) // 3, 1 + (k + 1) * (n_b - 1) // 3
+            lax.fori_loop(first, last, backward_step, 0)
+            turn()
+            if e == 0 and k == 1:
+                launch_out(1)
+        finish_units(e)
+    weight_part(E - 1, n_b - 1)
+    finish_expert(E - 1)
+    for copy in back:
+        copy.wait()
+    wb = sbuf.at[0:D, 2048 : 2048 + E * H]
 
     for k in range(4):
         v_mp[mp, 48 + k : 49 + k, :] = s2row[:, k * 128 : (k + 1) * 128]
@@ -680,27 +838,27 @@
             steps.append(step)
         return steps
 
-    queue.append(small_steps())
-
-    def input_gradient(i, carry):
-        r0 = pl.multiple_of(i * TB, TB)
-        lanes = pl.ds(r0, TB)
+    start_steps(small_steps(), 2)
+    turn()
+
+    def input_gradient(i):
+        lanes = pl.ds(i * TB, TB)
         da = zbuf[:, lanes]
         dl = dlogbuf[:, lanes]
         for k, half in ((0, mp), (1, other)):
             at = pl.ds(pl.multiple_of(half * 256, 256), 256)
             grad = nn(wb[at, :], da) + nn(gback[at, 0:16], dl)
             dobuf[k * H : (k + 1) * H, lanes] = grad.astype(BF16)
-        return carry
 
     n_c = R // TB
     for part in range(4):
-        lax.fori_loop(part * n_c // 4, (part + 1) * n_c // 4, input_gradient, 0)
-        turn()
+        for k in range(part * n_c // 4, (part + 1) * n_c // 4):
+            input_gradient(k)
+            turn()
         w = R // 4
         at = pl.ds(part * w, w)
         to = pl.ds(pl.multiple_of(mp * R + part * w, 128), w)
-        local = pltpu.make_async_copy(dobuf.at[0:H, at], d_hbm.at[:, to], sem_l.at[8 + part])
+        local = pltpu.make_async_copy(dobuf.at[0:H, at], d_hbm.at[:, to], sem_l.at[1 + NC + part])
         local.start()
         pending.append(local)
         pending.append(
@@ -713,64 +871,93 @@
 
 
 def final_kernel(
-    rows_tile, dt_ref, x_ref, v_ref, pred_ref, gout_ref, vout_ref, stat_ref,
-    o_pred, o_feat, o_in, o_inb, o_gain, o_nb, o_out, o_outb, o_gate, o_gateb,
+    tile, dt_hbm, x_hbm, v_ref, pred_ref, gout_ref, vout_ref, stat_ref,
+    o_pred, feat_hbm, o_in, o_inb, o_gain, o_nb, o_out, o_outb, o_gate, o_gateb,
     o_w1, o_b1, o_w2, o_b2, o_wl, o_bl,
+    dtb, xb, fb, sem_d, sem_x, sem_o,
 ):
     mp = lax.axis_index("mp")
+    rows = xb.shape[0]
     half = pl.ds(pl.multiple_of(mp * 256, 256), 256)
+    loads = []
+    for k in range(rows // tile):
+        at = pl.ds(k * tile, tile)
+        copies = (
+            pltpu.make_async_copy(dt_hbm.at[:, at], dtb.at[:, at], sem_d.at[k]),
+            pltpu.make_async_copy(x_hbm.at[at, half], xb.at[at, :], sem_x.at[k]),
+        )
+        for copy in copies:
+            copy.start()
+        loads.append(copies)
+
+    scale = 1.0 / stat_ref[2:3, 0:128]
+    one = scale[:, 0:1]
+    o_pred[...] = pred_ref[...]
+    for e in range(E):
+        for k in range(4):
+            g = gout_ref[e, (k // 2) * 128 : (k // 2 + 1) * 128, (k % 2) * 128 : (k % 2 + 1) * 128]
+            o_in[e, k * 128 : (k + 1) * 128, :] = (g.astype(F32) * one).T
+        for k in range(2):
+            g = gout_ref[TOWERS + 1 + e // 3, k * 128 : (k + 1) * 128, (e % 3) * 128 : (e % 3 + 1) * 128]
+            o_out[e, :, k * 128 : (k + 1) * 128] = g.astype(F32) * one
+        for ref, base in ((o_inb, 0), (o_gain, 12), (o_nb, 24)):
+            ref[e : e + 1, :] = vout_ref[pl.ds(base + 2 * e + mp, 1), :] * scale
+        for k in range(2):
+            o_outb[e : e + 1, k * 128 : (k + 1) * 128] = (
+                vout_ref[36 + 2 * e + k : 37 + 2 * e + k, :] * scale
+            )
+    o_w1[0] = gout_ref[TOWERS, :, 0:128].astype(F32) * one
+    o_w1[1] = gout_ref[TOWERS, :, 128:256].astype(F32) * one
+    g = gout_ref[TOWERS, 0:160, 256:384].astype(F32) * one
+    o_w2[0] = g[0:64]
+    o_w2[1] = g[64:128]
+    for k in range(4):
+        part = g[128 + 8 * k : 136 + 8 * k]
+        o_gate[0, :, k * 128 : (k + 1) * 128] = part[0:4]
+        o_gate[1, :, k * 128 : (k + 1) * 128] = part[4:8]
+    gate_bias = jnp.sum(vout_ref[52:60, :], axis=1, keepdims=True) * scale
+    table = jnp.concatenate([gate_bias, jnp.zeros((120, 128), F32)], axis=0).T
+    o_gateb[0:1, :] = table[0:1, 0:4]
+    o_gateb[1:2, :] = table[0:1, 4:8]
+    last = vout_ref[60:61, :] * scale
+    o_wl[0:1, :] = last[:, 0:64]
+    o_wl[1:2, :] = last[:, 64:128]
+    for t in range(2):
+        o_bl[t] = jnp.sum(vout_ref[61 + t : 62 + t, :] * scale)
+    o_b1[...] = vout_ref[63:65, :] * scale
+    b2 = vout_ref[65:66, :] * scale
+    o_b2[0:1, :] = b2[:, 0:64]
+    o_b2[1:2, :] = b2[:, 64:128]
+
     count = stat_ref[2:3, half]
     inv = stat_ref[1:2, half]
-    mu = stat_ref[0:1, half]
-    s1 = stat_ref[3:4, half] / count
-    s2 = stat_ref[4:5, half] / count
-    for at in range(0, rows_tile, 128):
-        valid = jnp.broadcast_to(v_ref[:, at : at + 128].astype(F32), (128, 128)).T
-        for k in range(2):
-            cols = slice(k * 128, (k + 1) * 128)
-            grad = dt_ref[cols, at : at + 128].astype(F32).T
-            xhat = (x_ref[at : at + 128, cols].astype(F32) - mu[:, cols]) * inv[:, cols]
-            o_feat[at : at + 128, cols] = inv[:, cols] * (
-                grad - valid * (s1[:, cols] + xhat * s2[:, cols])
-            )
-
-    @pl.when(pl.program_id(0) == 0)
-    def _():
-        scale = 1.0 / stat_ref[2:3, 0:128]
-        o_pred[...] = pred_ref[...]
-        for e in range(E):
-            g = gout_ref[e].astype(F32) * scale[:, 0:1]
-            for k in range(2):
-                o_in[e, k * 256 : k * 256 + 128, :] = g[k * 128 : (k + 1) * 128, 0:128].T
-                o_in[e, k * 256 + 128 : k * 256 + 256, :] = g[k * 128 : (k + 1) * 128, 128:256].T
-                o_out[e, :, k * 128 : (k + 1) * 128] = g[k * 128 : (k + 1) * 128, 256:384]
-            for ref, base in ((o_inb, 0), (o_gain, 12), (o_nb, 24)):
-                ref[e : e + 1, :] = vout_ref[pl.ds(base + 2 * e + mp, 1), :] * scale
-            for k in range(2):
-                o_outb[e : e + 1, k * 128 : (k + 1) * 128] = (
-                    vout_ref[36 + 2 * e + k : 37 + 2 * e + k, :] * scale
-                )
-        g = gout_ref[E].astype(F32) * scale[:, 0:1]
-        o_w1[0] = g[:, 0:128]
-        o_w1[1] = g[:, 128:256]
-        o_w2[0] = g[0:64, 256:384]
-        o_w2[1] = g[64:128, 256:384]
-        for k in range(4):
-            part = g[128 + 8 * k : 136 + 8 * k, 256:384]
-            o_gate[0, :, k * 128 : (k + 1) * 128] = part[0:4]
-            o_gate[1, :, k * 128 : (k + 1) * 128] = part[4:8]
-        gate_bias = jnp.sum(vout_ref[52:60, :], axis=1, keepdims=True) * scale
-        table = jnp.concatenate([gate_bias, jnp.zeros((120, 128), F32)], axis=0).T
-        o_gateb[0:1, :] = table[0:1, 0:4]
-        o_gateb[1:2, :] = table[0:1, 4:8]
-        last = vout_ref[60:61, :] * scale
-        o_wl[0:1, :] = last[:, 0:64]
-        o_wl[1:2, :] = last[:, 64:128]
-        o_bl[...] = jnp.sum(vout_ref[61:63, :], axis=1, keepdims=True) * scale
-        o_b1[...] = vout_ref[63:65, :] * scale
-        b2 = vout_ref[65:66, :] * scale
-        o_b2[0:1, :] = b2[:, 0:64]
-        o_b2[1:2, :] = b2[:, 64:128]
+    slope = inv * inv * (stat_ref[4:5, half] / count)
+    shift = inv * (stat_ref[3:4, half] / count) - stat_ref[0:1, half] * slope
+    eye = jnp.where(
+        lax.broadcasted_iota(jnp.int32, (256, 256), 0) == lax.broadcasted_iota(jnp.int32, (256, 256), 1), 1.0, 0.0
+    ).astype(BF16)
+    stores = []
+    for k in range(rows // tile):
+        for copy in loads[k]:
+            copy.wait()
+
+        def block(i, carry, k=k):
+            at = pl.ds(pl.multiple_of(k * tile + i * 256, 256), 256)
+            grad = nt(eye, dtb[:, at])
+            valid = nt(eye, jnp.broadcast_to(v_ref[:, at].astype(F32), (128, 256)).astype(BF16))
+            for c in range(2):
+                cols = slice(c * 128, (c + 1) * 128)
+                term = valid * (shift[:, cols] + xb[at, cols].astype(F32) * slope[:, cols])
+                fb[at, cols] = inv[:, cols] * grad[:, cols] - term
+            return carry
+
+        lax.fori_loop(0, tile // 256, block, 0, unroll=True)
+        at = pl.ds(k * tile, tile)
+        copy = pltpu.make_async_copy(fb.at[at, :], feat_hbm.at[at, :], sem_o.at[k])
+        copy.start()
+        stores.append(copy)
+    for copy in stores:
+        copy.wait()
 
 
 def on_device(
@@ -795,37 +982,39 @@
     def scr(*shape, dtype=F32):
         return pltpu.VMEM(shape, dtype)
 
+    low_rows = sum(p[2] for p in plan[1:]) + plan[-1][3]
     scratch = [
         scr(R, D, dtype=BF16), scr(E * H, R, dtype=BF16), scr(E * H, R, dtype=BF16),
         scr(E * H, R, dtype=BF16), scr(8, R), scr(16, R, dtype=BF16), scr(2, R),
-        scr(E * H + 32, D, dtype=BF16), scr(D, E * H, dtype=BF16), scr(D, 128, dtype=BF16),
-        scr(E * H, H, dtype=BF16), scr(E * H, H, dtype=BF16),
-        scr(E * H, 128), scr(E * H, 128), scr(E * H, 128), scr(E * H, 128), scr(E * H, 128),
+        scr(E * H + 32, D, dtype=BF16), scr(D, 128, dtype=BF16),
+        scr(E * H, H, dtype=BF16), scr(E * H, 128), scr(E * H, 128), scr(E * H, 128),
         scr(2, 128, H, dtype=BF16), scr(2, H, 128, dtype=BF16), scr(128, H, dtype=BF16),
         scr(H, 128, dtype=BF16), scr(H, 128), scr(128, 128), scr(128, 128), scr(8, 128),
-        scr(E * H, TF), scr(E * H, TF), scr(2 * H, TF, dtype=BF16), scr(H, TF, dtype=BF16), scr(2 * H, TF),
-        scr(H, D), scr(H, H), scr(16, D), scr(2, H, 128), scr(128, H),
-        scr(3, H, 128), scr(8, 128), scr(8, 128), scr(128, 128), scr(128, 128), scr(H, 128),
-        scr(1, D), scr(4, 8, H),
+        [scr(E * H, TF)] * 2, [scr(E * HE, TF, dtype=BF16)] * 2, [scr(8, TF)] * 2,
+        scr(2 * H, TF, dtype=BF16), scr(H, TF, dtype=BF16), scr(2 * H, TF),
+        scr(E * HE, H), scr(16, D), scr(2, H, 128), scr(128, H),
+        scr(8, 128), scr(8, 128), scr(128, 128), scr(128, 128), scr(H, 128), scr(1, D),
         scr(24, 128), scr(24, 128),
         scr(2, 8, D), scr(n_levels, 4, 8, D), scr(2, VR, 128), scr(n_levels, 4, VR, 128),
-        scr(2, H, CW), scr(NC, H, CW, dtype=BF16),
-        [scr(NC, radix, after, CW, dtype=BF16) for _, radix, _, after in plan],
+        scr(3, H, 384, dtype=BF16), scr(3, low_rows, 384, dtype=BF16),
+        [scr(H, w, dtype=BF16) for w in WIDTHS],
+        [[scr(radix, after, w, dtype=BF16) for _, radix, _, after in plan] for w in WIDTHS],
         dma((8,)), dma((8,)), dma((2 + 6 * n_levels,)), dma((2 + 6 * n_levels,)),
-        dma((NC, n_sems)), dma((NC, n_sems)), dma((12,)), dma((8,)),
+        dma((NC, n_sems)), dma((NC, n_sems)), dma((5 + NC,)), dma((8,)), dma((3 * E,)),
     ]
     flops = 2 * R * (6 * D * E * H // 2 + 3 * E * H * H)
-    d_half, preds, gsum, vsum, stats = pl.pallas_call(
+    d_half, preds, gsum, vsum, stats, _ = pl.pallas_call(
         functools.partial(main_kernel, plan, R),
         out_shape=(
             jax.ShapeDtypeStruct((256, rows), BF16),
             jax.ShapeDtypeStruct((2, rows), F32),
-            jax.ShapeDtypeStruct((NC, H, CW), BF16),
+            jax.ShapeDtypeStruct((NC, H, 384), BF16),
             jax.ShapeDtypeStruct((VR, 128), F32),
             jax.ShapeDtypeStruct((8, D), F32),
+            jax.ShapeDtypeStruct((2, D, E * 128), BF16),
         ),
-        in_specs=[hb] + [vm] * 9 + [sm] + [vm] * 5 + [sm],
-        out_specs=(hb, hb, hb, vm, vm),
+        in_specs=[hb] + [vm] * 2 + [hb] * 2 + [vm] * 5 + [sm] + [vm] * 5 + [sm],
+        out_specs=(hb, hb, hb, vm, vm, hb),
         scratch_shapes=scratch,
         compiler_params=pltpu.CompilerParams(
             collective_id=0, has_side_effects=True, vmem_limit_bytes=64 * 2**20 - 65536
@@ -838,27 +1027,22 @@
         jnp.swapaxes(tower_second, 1, 2), tower_second_bias, tower_last, tower_last_bias,
     )
 
-    tile = 512
-    whole = lambda *shape: pl.BlockSpec(shape, lambda i: (0,) * len(shape))
-    half_index = lambda i: (i, lax.axis_index("mp"))
+    tile = 1024
+    n_tiles = rows // tile
     out_shapes = [
         (2, rows), (rows, 256), (E, D, 128), (E, 128), (E, 128), (E, 128), (E, 128, H), (E, H),
-        (2, 4, D), (2, 4), (2, H, 128), (2, 128), (2, 64, 128), (2, 64), (2, 64), (2, 128),
+        (2, 4, D), (2, 4), (2, H, 128), (2, 128), (2, 64, 128), (2, 64), (2, 64), (2,),
     ]
-    out_specs = [whole(*shape) for shape in out_shapes]
-    out_specs[1] = pl.BlockSpec((tile, 256), lambda i: (i, 0))
     outs = pl.pallas_call(
         functools.partial(final_kernel, tile),
-        grid=(rows // tile,),
         out_shape=[jax.ShapeDtypeStruct(shape, F32) for shape in out_shapes],
-        in_specs=[
-            pl.BlockSpec((256, tile), lambda i: (0, i)),
-            pl.BlockSpec((tile, 256), half_index),
-            pl.BlockSpec((1, tile), lambda i: (0, i)),
-            whole(2, rows), whole(NC, H, CW), whole(VR, 128), whole(8, D),
+        in_specs=[hb, hb] + [vm] * 5,
+        out_specs=[vm, hb] + [vm] * 13 + [sm],
+        scratch_shapes=[
+            scr(256, rows, dtype=BF16), scr(rows, 256, dtype=BF16), scr(rows, 256),
+            dma((n_tiles,)), dma((n_tiles,)), dma((n_tiles,)),
         ],
-        out_specs=out_specs,
-        compiler_params=pltpu.CompilerParams(vmem_limit_bytes=48 * 2**20),
+        compiler_params=pltpu.CompilerParams(vmem_limit_bytes=64 * 2**20 - 65536),
         cost_estimate=pl.CostEstimate(
             flops=rows * 256 * 8, bytes_accessed=rows * 256 * 8, transcendentals=0
         ),
@@ -868,7 +1052,6 @@
     outs[0] = outs[0].T
     outs[8] = jnp.swapaxes(outs[8], 1, 2)
     outs[12] = jnp.swapaxes(outs[12], 1, 2)
-    outs[15] = outs[15][:, 0]
     return tuple(outs)
 
 

time: 164 us -> 144 us (0.88)
  Pallas kernels: 156 us -> 142 us
  local copies, waits for them, and re-layouts: 7.23 us -> 0 us
    pallas_call x1, Pallas kernels: 142 us -> 132 us  [on_device(): pl.pallas_call(functools.partial(main_kernel, plan, R), out_shape=(jax.Sh...]
    unnamed x12 -> x0, local copies, waits for them, and re-layouts: 6.6 us -> none
    pallas_call x1, Pallas kernels: 13.8 us -> 9.95 us  [on_device(): pl.pallas_call(functools.partial(final_kernel, tile), out_shape=[jax.Shap...]
where the time goes in v2:
time: 144 us; the launch traced here: 143 us
  Pallas kernels  142 us (99%)
    pallas_call x1, Pallas kernels, on_device(): pl.pallas_call(functools.partial(main_kernel, plan, R), out_shape=(jax.Sh...  132 us
    pallas_call x1, Pallas kernels, on_device(): pl.pallas_call(functools.partial(final_kernel, tile), out_shape=[jax.Shap...  9.95 us

profile of v2, /device:TPU:0, one launch (start us, length us, event | category | flops | bytes accessed | tf_op | source)
XLA Modules:
  0.0 142.7 jit_solution(7962810880416692150)
XLA Ops:
  0.7 131.9 %layer.1 = (bf16[256,8192]{1,0:T(8,128)(2,1)}, f32[2,8192]{1,0:T(2,128)}, bf16[9,256,384]{2,1,0:T(8,128)(2,1)}, f32[72,128]{1,0:T(8,128)}, f32[8,512]{1,0:T(8,128)}, /*index=5*/bf16[2,512,768]{2,1,0:T(8,128)(2,1)}) custom-call(bf16[8192,512]{1,0:T(8,128)(2,1)} %x_hbm.3, s32[1,8192]{1,0:T(1,128)} %bitcast.7, s32[2,8192]{1,0:T(2,128)} %bitcast.9, ...), custom_call_target="tpu_custom_call" | custom-call | flops 28991029248 | bytes 20971520 | tf_op jit(solution)/shard_map/layer/pallas_call | solution.py:1006
  132.5 10.0 %finish.1 = (f32[2,8192]{1,0:T(2,128)}, f32[8192,256]{1,0:T(8,128)}, f32[6,512,128]{2,1,0:T(8,128)}, f32[6,128]{1,0:T(8,128)}, f32[6,128]{1,0:T(8,128)}, /*index...) custom-call(bf16[256,8192]{1,0:T(8,128)(2,1)} %get-tuple-element.37., ...), custom_call_target="tpu_custom_call" | custom-call | flops 16777216 | bytes 16777216 | tf_op jit(solution)/shard_map/finish/pallas_call | solution.py:1036
